TPU v7x, 512 devices: a whole 4x8x8 slice. The times are simulated.
512 devices in a mesh: section: 8 (over z_hi, core), dp: 64 (over z_lo, y, x).
Axes of the slice: x: 4, y: 8, z: 8 (z_hi: 4, z_lo: 2; z = z_hi * 2 + z_lo), core: 2. Of those that a mesh axis runs over, the one named last changes fastest.
Arguments:
- patches: bfloat16 [4096, 8, 3200], P('dp'), may hold values from -6 to 6
- tile_counts: int32 [512], P('dp'), may hold values from 1 to 8, as said below
- owners: int32 [4096, 1], P('dp'), may hold values from 0 to 63; in each aligned block of 64 rows (0 to 63, 64 to 127, ...) at most 2 rows name the same one
- plan: int32 [8, 4], replicated, may hold values from 0 to 31, as said below
- norm_gain: float32 [3200], replicated, may hold values from 0.25 to 1.75
- fc1_weight: bfloat16 [3200, 6400], P('dp', 'section'), may hold values from -0.109375 to 0.109375
- fc1_bias: float32 [6400], replicated, may hold values from -4 to 4
- fc2_weight: bfloat16 [6400, 3200], P('section', 'dp'), may hold values from -0.078125 to 0.078125
- fc2_bias: float32 [3200], replicated, may hold values from -3 to 3
- layer_scale: float32 [3200], replicated, may hold values from 0.3 to 3
Outputs:
- received: bfloat16 [65536, 3200], P('dp', 'section')
Inputs may be any that keep to these rules, and one draw needn't show every extreme that they name: `tile_counts`: every dp index has an image with 8 tiles. `owners`: at most 2 tile slots of one dp index name one owner. `plan`: a permutation of the hidden-unit blocks.
All inputs are finite; a program needn't handle non-finite values.
Results may differ from a plain program's by a relative error of at most 0.015.
Values may be sent and summed in bfloat16 or wider, within the bound.
A program may use at most 128 MiB of HBM per device.

v0:
```python
import jax
import jax.numpy as jnp
from jax import lax
from jax.sharding import PartitionSpec as P


def local(
    patches,
    tile_counts,
    owners,
    plan,
    norm_gain,
    fc1_weight,
    fc1_bias,
    fc2_weight,
    fc2_bias,
    layer_scale,
):
    tiles_dev, tile_rows, width = patches.shape
    n_section = lax.axis_size("section")
    n_dp = lax.axis_size("dp")
    section_id = lax.axis_index("section")
    ff_section = fc1_weight.shape[1]
    slots = plan.shape[1]
    n_blocks = plan.shape[0] * slots
    block_width = ff_section // slots
    feat = width // n_section
    capacity = max(2, (tiles_dev + n_dp - 1) // n_dp)
    total_rows = tiles_dev * tile_rows
    my_blocks = lax.dynamic_slice_in_dim(plan, section_id, 1, 0)[0]
    picker = (my_blocks[:, None] == jnp.arange(n_blocks, dtype=jnp.int32)[None, :]).astype(
        jnp.float32
    )
    loc_bias = jnp.dot(
        picker, fc1_bias.reshape(n_blocks, block_width), precision=lax.Precision.HIGHEST
    ).reshape(ff_section)
    images = tile_counts.shape[0]
    per_image = tiles_dev // images
    tile_live = (jnp.arange(per_image)[None, :] < tile_counts[:, None]).reshape(tiles_dev)
    owner = owners[:, 0]
    same = owner[:, None] == owner[None, :]
    earlier = jnp.arange(tiles_dev)[:, None] > jnp.arange(tiles_dev)[None, :]
    rank = jnp.sum((same & earlier).astype(jnp.int32), axis=1)
    target = owner * capacity + rank
    rows = patches.reshape(total_rows, width)
    values = rows.astype(jnp.float32)
    scale = lax.rsqrt(jnp.mean(values * values, axis=1, keepdims=True) + 1e-06)
    normed = (values * scale * norm_gain).astype(jnp.bfloat16)
    term = jnp.dot(
        normed,
        lax.all_gather(fc1_weight, "dp", axis=0, tiled=True),
        preferred_element_type=jnp.float32,
    )
    hidden = jax.nn.gelu(term + loc_bias, approximate=False).astype(jnp.bfloat16)
    partial_sums = jnp.dot(
        hidden,
        lax.all_gather(fc2_weight, "dp", axis=1, tiled=True),
        preferred_element_type=jnp.float32,
    )
    summed = lax.psum(partial_sums.astype(jnp.bfloat16), "section").astype(jnp.float32)
    branch = lax.dynamic_slice_in_dim(summed, section_id * feat, feat, 1)
    start = section_id * feat
    own_values = lax.dynamic_slice_in_dim(values, start, feat, 1)
    own_bias = lax.dynamic_slice_in_dim(fc2_bias, start, feat, 0)
    own_scale = lax.dynamic_slice_in_dim(layer_scale, start, feat, 0)
    keep = jnp.repeat(tile_live, tile_rows).astype(jnp.float32)[:, None]
    encoded = ((own_values + own_scale * (branch + own_bias)) * keep).astype(jnp.bfloat16)
    placing = (jnp.arange(n_dp * capacity, dtype=jnp.int32)[:, None] == target[None, :]).astype(
        jnp.bfloat16
    )
    outgoing = jnp.dot(
        placing, encoded.reshape(tiles_dev, tile_rows * feat), preferred_element_type=jnp.float32
    )
    outgoing = outgoing.astype(jnp.bfloat16).reshape(n_dp, capacity * tile_rows, feat)
    incoming = lax.all_to_all(outgoing, "dp", split_axis=0, concat_axis=0, tiled=True)
    return incoming.reshape(n_dp * capacity * tile_rows, feat)


def solution(mesh):
    in_specs = (
        P("dp", None, None),
        P("dp"),
        P("dp", None),
        P(),
        P(),
        P("dp", "section"),
        P(),
        P("section", "dp"),
        P(),
        P(),
    )
    out_specs = P("dp", "section")
    return jax.shard_map(local, mesh=mesh, in_specs=in_specs, out_specs=out_specs, check_vma=False)
```

profile of v0, /device:TPU:6, one launch (start us, length us, event | category | flops | bytes accessed | tf_op | source)
XLA Modules:
  0.0 814.5 jit_solution(8182123422727729238)
XLA Ops:
  6.5 0.7 all-gather.5.cloned.1.call-update
  7.3 0.7 all-gather.7.cloned.1.call-update
  8.1 0.8 reshape.60
  8.9 0.2 dynamic-slice_reduce_fusion
  9.1 0.2 fusion.43
  9.4 2.7 fusion
  12.1 307.0 %all-gather.5.cloned.1.call-done = bf16[64,50,800]{2,1,0:T(8,128)(2,1)} async-done(((bf16[1,50,800]{2,1,0:T(8,128)(2,1)}), bf16[64,50,800]{2,1,0:T(8,128)(2,1)}) %all-gather.5.cloned.1.call-update) | async-done | bytes 5120016 | tf_op jit(solution)/shard_map/all_gather | solution.py:51
  319.2 8.6 %reshape.67 = bf16[3200,800]{1,0:T(8,128)(2,1)} reshape(bf16[64,50,800]{2,1,0:T(8,128)(2,1)} %all-gather.5.cloned.1.call-done) | data formatting | bytes 10240000
  327.8 301.4 %all-gather.7.cloned.1.call-done = bf16[64,50,800]{2,1,0:T(8,128)(2,1)} async-done(((bf16[1,50,800]{2,1,0:T(8,128)(2,1)}), bf16[64,50,800]{2,1,0:T(8,128)(2,1)}) %all-gather.7.cloned.1.call-update) | async-done | bytes 5120016 | tf_op jit(solution)/shard_map/all_gather | solution.py:57
  629.2 8.6 %reshape.69 = bf16[3200,800]{1,0:T(8,128)(2,1)} reshape(bf16[64,50,800]{2,1,0:T(8,128)(2,1)} %all-gather.7.cloned.1.call-done) | data formatting | bytes 10240000
  637.9 15.6 %convolution_convert_fusion = bf16[512,3200]{0,1:T(8,128)(2,1)} fusion(bf16[3200,800]{1,0:T(8,128)(2,1)} %reshape.69, bf16[3200,800]{1,0:T(8,128)(2,1)} %reshape.67, f32[3200]{0:T(1024)S(1)} %copy-done.3, f32[512]{0:T(512)S(1)} %rsqrt.12, bf16[64,8,3200]{2,1,0:T(8,128)(2,1)S(1)} %copy-done.1, f32[800]{0:T(1024)S(1)} %add.56), kind=kOutput, calls=%fused_computation.4 | convolution fusion | flops 5278105600 | bytes 16811648 | tf_op jit(solution)/shard_map/dot_general | solution.py:55
  653.4 0.8 dynamic_slice.19
  654.2 0.8 dynamic_slice.16
  655.3 0.5 convert_bitcast_fusion
  655.8 0.3 constant_dynamic-slice_fusion
  656.1 0.3 copy.22
  656.6 106.5 %all-reduce.2.cloned.1.call-done = bf16[512,3200]{0,1:T(8,128)(2,1)} async-done(((bf16[512,3200]{0,1:T(8,128)(2,1)}), bf16[512,3200]{0,1:T(8,128)(2,1)}) %all-reduce.2.cloned.1.call-update) | async-done | bytes 3276816 | tf_op jit(solution)/shard_map/psum | solution.py:60
  763.1 1.2 multiply_convert_fusion.4
  764.4 0.2 copy.20
  764.6 0.6 reshape.61
  765.2 0.5 convolution_convert_fusion.1
  765.8 2.3 reshape.62
  768.1 38.7 %all_to_all.5 = bf16[64,16,400]{2,1,0:T(8,128)(2,1)S(1)} all-to-all(bf16[64,16,400]{2,1,0:T(8,128)(2,1)S(1)} %reshape.62), channel_id=1, replica_groups=mesh['section'=8,'dp'=64] {'dp'}, dimensions={0} | all-to-all | bytes 1638400 | tf_op jit(solution)/shard_map/all_to_all | solution.py:75
  806.8 1.2 copy.21
  (23 shorter events, 0.8 us)
Async XLA Ops:
  6.5 2.4 copy-start
  6.5 312.6 %all-gather.5.cloned.1.call-start = ((), (), s32[]{:S(2)}) async-start(), calls=%async_computation.2 | async-start | bytes 6522880 | tf_op jit(solution)/shard_map/all_gather | solution.py:51
  7.3 621.9 %all-gather.7.cloned.1.call-start = ((), (), s32[]{:S(2)}) async-start(), calls=%async_computation.3 | async-start | bytes 6522880 | tf_op jit(solution)/shard_map/all_gather | solution.py:57
  8.0 755.1 %all-reduce.2.cloned.1.call-start = ((), (), s32[]{:S(2)}) async-start(), calls=%async_computation.1 | async-start | bytes 6553600 | tf_op jit(solution)/shard_map/psum | solution.py:60
  327.8 310.1 %copy-start.1 = (bf16[64,8,3200]{2,1,0:T(8,128)(2,1)S(1)}, bf16[64,8,3200]{2,1,0:T(8,128)(2,1)}, u32[]{:S(2)}) copy-start(bf16[64,8,3200]{2,1,0:T(8,128)(2,1)} %param.10) | copy-start | bytes 9830404
  327.8 310.1 %copy-start.3 = (f32[3200]{0:T(1024)S(1)}, f32[3200]{0:T(1024)}, u32[]{:S(2)}) copy-start(f32[3200]{0:T(1024)} %param.14) | copy-start | bytes 38404
  653.4 1.6 copy-start.2
  655.8 0.7 copy-start.4
Sparse Core Ops, SparseCore 0:
  9.4 309.6 all-gather.4
  321.2 307.9 all-gather.6
  653.6 109.5 all-reduce.1
where the time goes:
time: 815 us
  waiting for transfers between devices  716 us (88%)
  blocking collectives  38.7 us (5%)
  local copies, waits for them, and re-layouts  25.3 us (3%)
  matrix products  16.3 us (2%)
  between operations  13.2 us (2%)
    all_gather x1, waiting for transfers between devices, local(): lax.all_gather(fc1_weight, 'dp', axis=0, tiled=True)  307 us
    all_gather x1, waiting for transfers between devices, local(): lax.all_gather(fc2_weight, 'dp', axis=1, tiled=True)  301 us
    psum x1, waiting for transfers between devices, local(): lax.psum(partial_sums.astype(jnp.bfloat16), 'section').astype(jnp.float32)  107 us
    all_to_all x1, blocking collectives, local(): lax.all_to_all(outgoing, 'dp', split_axis=0, concat_axis=0, tiled=True)  38.7 us
    unnamed x13, local copies, waits for them, and re-layouts  17.6 us
  transfers between devices with their start and end apart: 3, of which 3 were waited for; matrix products, arithmetic and copies ran while one was open for 2% of the time, Pallas kernels for 0%

commit v1 on v0

v1 whole, which is shorter than its diff:
```python
import jax
import jax.numpy as jnp
from jax import lax
from jax.experimental import pallas as pl
from jax.experimental.pallas import tpu as pltpu
from jax.sharding import PartitionSpec as P

MESH = pl.DeviceIdType.MESH
F32 = jnp.float32
BF16 = jnp.bfloat16

NQ, NC, NZ, NY, NX = 4, 2, 2, 8, 4
NS = NQ * NC
D = 3200
FF = 800
FP = 896
SH = 50
SHP = 64
RUN = 200
RUNP = 208
FEAT = 400
ROWS = 512
TOK = 256
CUTS = ((0, 512), (512, 384))


def md(a, n):
    return lax.rem(a, jnp.int32(n))


def dv(a, n):
    return lax.div(a, jnp.int32(n))


def dot(a, b, dims=((1,), (0,))):
    return lax.dot_general(a, b, (dims, ((), ())), preferred_element_type=F32)


def iota(shape, dim):
    return lax.broadcasted_iota(jnp.int32, shape, dim)


def window(start):
    block = dv(start, 128) - dv(start, 3000)
    return pl.multiple_of(block * 128, 128), start - block * 128


def kernel(
    patches,
    gain,
    w1,
    w2,
    loc_bias,
    own_scale,
    own_bias,
    target,
    out,
    own,
    stage,
    wall,
    normed,
    acts,
    acc,
    hidden,
    part,
    pair,
    ring_out,
    ring_in,
    branch,
    encoded,
    going,
    coming,
    turned,
    st_send,
    st_recv,
    y_send,
    y_recv,
    x_send,
    x_recv,
    c_send,
    c_recv,
    r_send,
    r_recv,
    a_send,
    a_recv,
    b_send,
    b_recv,
):
    s = lax.axis_index("section")
    d = lax.axis_index("dp")
    q, c = dv(s, 2), md(s, 2)
    z, y, x = dv(d, 32), md(dv(d, 4), 8), md(d, 4)
    h = md(x, 2)
    e = md(x + z, 2)

    def dp_id(z_, y_, x_):
        return (s, z_ * 32 + y_ * 4 + x_)

    def peer(step):
        g = md(z * 4 + x + step, 8)
        return g, dv(g, 4), md(g, 4)

    def copy(src, dst, send, recv, device):
        return pltpu.make_async_remote_copy(
            src_ref=src,
            dst_ref=dst,
            send_sem=send,
            recv_sem=recv,
            device_id=device,
            device_id_type=MESH,
        )

    mate = (q * 2 + 1 - c, d)
    q_up = (md(q + 1, NQ) * 2 + c, d)
    q_dn = (md(q + NQ - 1, NQ) * 2 + c, d)

    barrier = pltpu.get_barrier_semaphore()
    for step in range(1, 8):
        _, zp, xp = peer(step)
        for device in (dp_id(zp, y, xp), dp_id(z, md(y + step, 8), x)):
            pl.semaphore_signal(barrier, inc=1, device_id=device, device_id_type=MESH)
    for device in (mate, q_up, q_dn):
        pl.semaphore_signal(barrier, inc=1, device_id=device, device_id_type=MESH)

    own[...] = jnp.zeros_like(own)
    own[0, 0:SH, 0:FF] = w1[...]
    eye = (iota((SHP, SH), 0) == iota((SHP, SH), 1)).astype(BF16)
    own[1, :, 0:FF] = dot(eye, w2[...], ((1,), (1,))).astype(BF16)

    pl.semaphore_wait(barrier, 17)

    def stage_copy(m, k, l):
        return copy(
            own.at[m],
            stage.at[m, x],
            st_send.at[m, 2 * k + l],
            st_recv.at[m, x],
            dp_id(md(z + l, 2), y, md(x + e + 2 * k, 4)),
        )

    def stage_start(m):
        for k in range(2):
            for l in range(2):
                if k or l:
                    stage_copy(m, k, l).start()
        pl.when(e == 1)(lambda: stage_copy(m, 0, 0).start())

        @pl.when(e == 0)
        def _():
            stage[m, x] = own[m]

    def stage_arrive(m, j):
        xs = md(x + j, 4)
        copy(own.at[m], stage.at[m, xs], st_send.at[m, 0], st_recv.at[m, xs], dp_id(z, y, x)).wait_recv()

    def stage_finish(m):
        pl.when(e == 1)(lambda: stage_arrive(m, 0))
        for j in range(1, 4):
            stage_arrive(m, j)
        row, col = iota((RUNP, 4 * SHP), 0), iota((RUNP, 4 * SHP), 1)
        pick = ((col == dv(row, SH) * SHP + md(row, SH)) & (row < RUN)).astype(BF16)
        wall[m, y, h] = dot(pick, stage[m].reshape(4 * SHP, FP)).astype(BF16)

    def y_copy(m, way, t, arriving=False):
        back = t + 1 if arriving else t
        b = md(y + 8 - back, 8) if way == 0 else md(y + back, 8)
        to = md(y + 1, 8) if way == 0 else md(y + 7, 8)
        start, size = (0, FP) if t < 3 else CUTS[way]
        ref = wall.at[m, b, h, :, pl.ds(start, size)]
        return copy(ref, ref, y_send.at[m, way, t], y_recv.at[m, way, t], dp_id(z, to, x))

    def x_copy(m, way, b, arriving=False):
        to = md(x + 1, 4) if way == 0 else md(x + 3, 4)
        half = 1 - h if arriving else h
        ref = wall.at[m, b, half, :, pl.ds(CUTS[way][0], CUTS[way][1])]
        return copy(ref, ref, x_send.at[m, way, b], x_recv.at[m, way, b], dp_id(z, y, to))

    def block_at(way, t):
        return md(y + 8 - t, 8) if way == 0 else md(y + t, 8)

    def send_block(m, t):
        for way in range(2):
            if t > 0:
                y_copy(m, way, t - 1, True).wait_recv()
            if t < 4:
                y_copy(m, way, t).start()
            if t in (0, 4):
                x_copy(m, way, block_at(way, t)).start()
            else:
                for other in range(2):
                    x_copy(m, other, block_at(way, t)).start()

    def use_block(m, t, use):
        def one(way, carry):
            b = md(y + way * t + (1 - way) * (8 - t), 8)
            for other in range(2):
                x_copy(m, other, b, True).wait_recv()
            use(b)
            return carry

        lax.fori_loop(0, 1 if t in (0, 4) else 2, one, 0)

    def fc1(b):
        acc[...] += dot(acts[b], wall[0, b].reshape(2 * RUNP, FP))

    def fc2(b):
        term = dot(wall[1, b].reshape(2 * RUNP, FP), hidden[...], ((1,), (1,))).astype(BF16)
        term = term.reshape(2, RUNP, ROWS)
        sec, j = dv(b, 2), md(b, 2)
        part[sec, j] = term[0]
        part[sec + 4, j] = term[1]

    stage_start(0)
    stage_start(1)

    def norm(i, carry):
        at = pl.ds(pl.multiple_of(i * 64, 64), 64)
        values = patches[at, :].astype(F32)
        scale = lax.rsqrt(jnp.mean(values * values, axis=1, keepdims=True) + 1e-06)
        normed[at, :] = (values * scale * gain[...]).astype(BF16)
        return carry

    def act(b, carry):
        total = None
        for half in range(2):
            at, off = window(half * 1600 + b * RUN)
            row, col = iota((384, 2 * RUNP), 0), iota((384, 2 * RUNP), 1) - half * RUNP
            pick = ((row == col + off) & (col >= 0) & (col < RUN)).astype(BF16)
            term = dot(normed[:, pl.ds(at, 384)], pick)
            total = term if total is None else total + term
        acts[b] = total.astype(BF16)
        return carry

    stage_finish(0)
    send_block(0, 0)
    lax.fori_loop(0, 8, norm, 0)
    lax.fori_loop(0, 8, act, 0)
    acc[...] = jnp.zeros_like(acc)
    stage_finish(1)
    send_block(0, 1)
    send_block(1, 0)
    use_block(0, 0, fc1)
    send_block(0, 2)
    use_block(0, 1, fc1)
    send_block(1, 1)
    send_block(0, 3)
    use_block(0, 2, fc1)
    send_block(0, 4)
    use_block(0, 3, fc1)
    send_block(1, 2)
    use_block(0, 4, fc1)

    def gelu(i, carry):
        at = pl.ds(pl.multiple_of(i * 64, 64), 64)
        pre = acc[at, :] + loc_bias[...]
        hidden[at, :] = (0.5 * pre * (1.0 + lax.erf(pre * 0.7071067811865476))).astype(BF16)
        return carry

    lax.fori_loop(0, 8, gelu, 0)
    use_block(1, 0, fc2)
    send_block(1, 3)
    use_block(1, 1, fc2)
    use_block(1, 2, fc2)
    send_block(1, 4)
    use_block(1, 3, fc2)
    use_block(1, 4, fc2)

    def pair_copy(i):
        return copy(part.at[2 * i + 1 - c], pair.at[i], c_send.at[i], c_recv.at[i], mate)

    for i in range(NQ):
        pair_copy(i).start()

    def chunk(i, way):
        at = slice(way * TOK, way * TOK + TOK)
        return part[2 * i + c, :, :, at].astype(F32) + pair[i, :, :, at].astype(F32)

    def ring_copy(way, k):
        return copy(
            ring_out.at[way, k],
            ring_in.at[way, k],
            r_send.at[way, k],
            r_recv.at[way, k],
            q_up if way == 0 else q_dn,
        )

    for i in range(NQ):
        pair_copy(i).wait()
    for k in range(4):
        for way in range(2):
            i = md(q + 7 - k, NQ) if way == 0 else md(q + 1 + k, NQ)
            total = chunk(i, way)
            if k > 0:
                ring_copy(way, k - 1).wait_recv()
                total = total + ring_in[way, k - 1].astype(F32)
            if k < 3:
                ring_out[way, k] = total.astype(BF16)
                ring_copy(way, k).start()
            else:
                branch[:, :, way * TOK : way * TOK + TOK] = total

    for j in range(2):
        at, off = window(s * FEAT + j * RUN)
        row, col = iota((RUNP, 384), 0), iota((RUNP, 384), 1)
        pick = ((col == row + off) & (row < RUN)).astype(BF16)
        rows = dot(pick, patches[:, pl.ds(at, 384)], ((1,), (1,)))
        encoded[j * RUNP : (j + 1) * RUNP] = (
            rows + own_scale[j] * (branch[j] + own_bias[j])
        ).astype(BF16)

    def place(b, carry):
        pick = (target[...] == iota((ROWS, 128), 1) + b * 128).astype(BF16)
        going[b] = dot(encoded[...], pick).astype(BF16)
        return carry

    lax.fori_loop(0, 8, place, 0)

    def a_copy(step, arriving=False):
        to = md(y + step, 8)
        src = md(y + 8 - step, 8) if arriving else y
        return copy(going.at[to], coming.at[src], a_send.at[step], a_recv.at[step], dp_id(z, to, x))

    for step in (4, 3, 5, 2, 6, 1, 7):
        a_copy(step).start()

    row, col = iota((2 * RUNP, FEAT), 0), iota((2 * RUNP, FEAT), 1)
    keep = (row == col + jnp.where(col >= RUN, RUNP - RUN, 0)).astype(BF16)

    def turn(src, block):
        turned[:, src] = dot(block, keep, ((0,), (0,))).astype(BF16).reshape(8, 16, FEAT)

    turn(y, going[y])
    for step in (1, 7, 2, 6, 3, 5, 4):
        a_copy(step, True).wait_recv()
        src = md(y + 8 - step, 8)
        turn(src, coming[src])

    def b_copy(step, arriving=False):
        g, zp, xp = peer(8 - step) if arriving else peer(step)
        zo, xo = (zp, xp) if arriving else (z, x)
        return copy(turned.at[g], out.at[zo, :, xo], b_send.at[step], b_recv.at[step], dp_id(zp, y, xp))

    for step in range(1, 8):
        b_copy(step).start()
    out[z, :, x] = turned[z * 4 + x]
    for step in range(1, 8):
        b_copy(step, True).wait_recv()

    for m in range(2):
        for k in range(2):
            for l in range(2):
                if k or l:
                    stage_copy(m, k, l).wait_send()
        pl.when(e == 1)(lambda: stage_copy(m, 0, 0).wait_send())
        for way in range(2):
            for t in range(4):
                y_copy(m, way, t).wait_send()
            for b in range(8):
                x_copy(m, way, b).wait_send()
    for way in range(2):
        for k in range(3):
            ring_copy(way, k).wait_send()
    for step in range(1, 8):
        a_copy(step).wait_send()
        b_copy(step).wait_send()


def local(
    patches,
    tile_counts,
    owners,
    plan,
    norm_gain,
    fc1_weight,
    fc1_bias,
    fc2_weight,
    fc2_bias,
    layer_scale,
):
    tiles, tile_rows, width = patches.shape
    section_id = lax.axis_index("section")
    blocks = plan.shape[0] * plan.shape[1]
    my_blocks = lax.dynamic_slice_in_dim(plan, section_id, 1, 0)[0]
    loc_bias = jnp.take(fc1_bias.reshape(blocks, -1), my_blocks, axis=0).reshape(1, FF)
    loc_bias = jnp.pad(loc_bias, ((0, 0), (0, FP - FF)))

    per_image = tiles // tile_counts.shape[0]
    live = (jnp.arange(per_image)[None, :] < tile_counts[:, None]).reshape(tiles)
    owner = owners[:, 0]
    same = owner[:, None] == owner[None, :]
    earlier = jnp.arange(tiles)[:, None] > jnp.arange(tiles)[None, :]
    rank = jnp.sum((same & earlier).astype(jnp.int32), axis=1)
    oz, oy, ox = owner // 32, (owner // 4) % 8, owner % 4
    place = oy * 128 + (oz * 4 + ox) * 16 + rank * 8
    target = place[:, None] + jnp.arange(tile_rows, dtype=jnp.int32)[None, :]
    target = jnp.where(live[:, None], target, -1).reshape(ROWS, 1)

    def mine(vector):
        held = lax.dynamic_slice_in_dim(vector, section_id * FEAT, FEAT, 0).reshape(2, RUN, 1)
        return jnp.pad(held, ((0, 0), (0, RUNP - RUN), (0, 0)))

    vmem = pl.BlockSpec(memory_space=pltpu.VMEM)
    dma = pltpu.SemaphoreType.DMA
    received = pl.pallas_call(
        kernel,
        out_shape=jax.ShapeDtypeStruct((NZ, NY, NX, 16, FEAT), BF16),
        in_specs=[vmem] * 8,
        out_specs=vmem,
        scratch_shapes=[
            pltpu.VMEM((2, SHP, FP), BF16),
            pltpu.VMEM((2, 4, SHP, FP), BF16),
            pltpu.VMEM((2, 8, 2, RUNP, FP), BF16),
            pltpu.VMEM((ROWS, D), BF16),
            pltpu.VMEM((8, ROWS, 2 * RUNP), BF16),
            pltpu.VMEM((ROWS, FP), F32),
            pltpu.VMEM((ROWS, FP), BF16),
            pltpu.VMEM((NS, 2, RUNP, ROWS), BF16),
            pltpu.VMEM((NQ, 2, RUNP, ROWS), BF16),
            pltpu.VMEM((2, 3, 2, RUNP, TOK), BF16),
            pltpu.VMEM((2, 3, 2, RUNP, TOK), BF16),
            pltpu.VMEM((2, RUNP, ROWS), F32),
            pltpu.VMEM((2 * RUNP, ROWS), BF16),
            pltpu.VMEM((8, 2 * RUNP, 128), BF16),
            pltpu.VMEM((8, 2 * RUNP, 128), BF16),
            pltpu.VMEM((8, 8, 16, FEAT), BF16),
            dma((2, 4)),
            dma((2, 4)),
            dma((2, 2, 4)),
            dma((2, 2, 4)),
            dma((2, 2, 8)),
            dma((2, 2, 8)),
            dma((4,)),
            dma((4,)),
            dma((2, 3)),
            dma((2, 3)),
            dma((8,)),
            dma((8,)),
            dma((8,)),
            dma((8,)),
        ],
        compiler_params=pltpu.CompilerParams(
            collective_id=0, has_side_effects=True, vmem_limit_bytes=56 * 1024 * 1024
        ),
    )(
        patches.reshape(ROWS, width),
        norm_gain.reshape(1, width),
        fc1_weight,
        fc2_weight,
        loc_bias,
        mine(layer_scale),
        mine(fc2_bias),
        target,
    )
    return received.reshape(NZ * NY * NX * 16, FEAT)


def solution(mesh):
    in_specs = (
        P("dp", None, None),
        P("dp"),
        P("dp", None),
        P(),
        P(),
        P("dp", "section"),
        P(),
        P("section", "dp"),
        P(),
        P(),
    )
    out_specs = P("dp", "section")
    return jax.shard_map(local, mesh=mesh, in_specs=in_specs, out_specs=out_specs, check_vma=False)
```

time: 815 us -> 197 us (0.24)
  waiting for transfers between devices: 716 us -> 0 us
  Pallas kernels: 0 us -> 182 us
  blocking collectives: 38.7 us -> 0 us
  matrix products: 16.3 us -> 0 us
  between operations: 13.2 us -> 0.06 us
  local copies, waits for them, and re-layouts: 25.3 us -> 12.5 us
    all_gather x2 -> x0, waiting for transfers between devices: 608 us -> none  [the longest x1 307 us: local(): lax.all_gather(fc1_weight, 'dp', axis=0, tiled=True)]
    pallas_call x0 -> x1, Pallas kernels: none -> 182 us  [local(): pl.pallas_call(kernel, out_shape=jax.ShapeDtypeStruct((NZ, NY, NX, 16, FE...]
    psum x1 -> x0, waiting for transfers between devices: 107 us -> none  [local(): lax.psum(partial_sums.astype(jnp.bfloat16), 'section').astype(jnp.float32)]
    all_to_all x1 -> x0, blocking collectives: 38.7 us -> none  [local(): lax.all_to_all(outgoing, 'dp', split_axis=0, concat_axis=0, tiled=True)]
    dot_general x3 -> x0, matrix products: 16.3 us -> none  [the longest x1 15.6 us: local(): jnp.dot(hidden, lax.all_gather(fc2_weight, 'dp', axis=1, tiled=True), pre...]
    unnamed x13 -> x3, local copies, waits for them, and re-layouts: 17.6 us -> 2.39 us
  transfers between devices with their start and end apart: 3 -> 0, of which waited for: 3 -> 0; matrix products, arithmetic and copies ran while one was open for 2% -> 0% of each run, Pallas kernels for 0% -> 0%
where the time goes in v1:
time: 197 us
  Pallas kernels  182 us (92%)
  local copies, waits for them, and re-layouts  12.5 us (6%)
  other arithmetic  2.49 us (1%)
    pallas_call x1, Pallas kernels, local(): pl.pallas_call(kernel, out_shape=jax.ShapeDtypeStruct((NZ, NY, NX, 16, FE...  182 us

profile of v1, /device:TPU:6, one launch (start us, length us, event | category | flops | bytes accessed | tf_op | source)
XLA Modules:
  0.0 196.8 jit_solution(1293434432075350010)
XLA Ops:
  0.0 0.0 copy-start
  0.0 0.7 copy-done
  0.7 0.2 dynamic-slice_reduce_fusion
  0.9 0.9 convert_reduce_fusion
  1.8 0.7 fusion.7
  2.5 0.7 iota_compare_fusion.1
  3.2 0.1 lt.59
  3.3 0.8 dynamic_slice.11
  4.1 0.8 dynamic_slice.10
  4.8 1.3 reshape.137.gain
  6.2 0.1 add_select_fusion
  6.3 0.8 reshape.138
  7.1 0.6 gather_fusion
  7.7 0.1 broadcast_select_fusion
  7.7 0.1 select_n.78
  7.8 0.6 pad.11.loc_bias
  8.4 0.2 reshape.150
  8.7 0.7 pad.12.own_scale
  9.4 0.2 reshape.151
  9.6 0.7 pad.13.own_bias
  10.3 1.7 copy.20.w2
  12.0 0.8 select_n.86.target
  12.8 181.8 %shard_map.100 = bf16[2,8,4,16,400]{4,3,2,1,0:T(8,128)(2,1)} custom-call(bf16[512,3200]{1,0:T(8,128)(2,1)} %bitcast.14, f32[1,3200]{1,0:T(1,128)} %reshape.137.gain, bf16[50,800]{1,0:T(8,128)(2,1)} %w1.1, bf16[800,50]{1,0:T(8,128)(2,1)} %copy.20.w2, f32[1,896]{1,0:T(1,128)} %pad.11.loc_bias, f32[2,208,1]{2,1,0:T(8,128)} %pad.12.own_scale, ...), custom_call_target="tpu_custom_call" | custom-call | tf_op jit(solution)/shard_map/pallas_call | solution.py:404
  194.6 2.2 %copy.22 = bf16[1024,400]{0,1:T(8,128)(2,1)} copy(bf16[1024,400]{1,0:T(8,128)(2,1)} %bitcast.13) | data formatting | bytes 1638400 | tf_op jit(solution)/shard_map/reshape | solution.py:454
  (3 shorter events, 0.0 us)
Async XLA Ops:
  0.0 0.7 copy-start

commit v2 on v1

v2 whole, which is shorter than its diff:
```python
import jax
import jax.numpy as jnp
from jax import lax
from jax.experimental import pallas as pl
from jax.experimental.pallas import tpu as pltpu
from jax.sharding import PartitionSpec as P

MESH = pl.DeviceIdType.MESH
F32 = jnp.float32
BF16 = jnp.bfloat16

NQ, NZ, NY, NX = 4, 2, 8, 4
D = 3200
FF = 800
FP = 896
SLOT = 200
SH = 50
SHP = 64
RUN = 200
RUNP = 208
FEAT = 400
ROWS = 512
TILES = 64
TOK = 256
Y_CUTS = ((0, 512), (512, 384))
X_CUTS = (
    ((0, 384), (384, 256), (640, 256)),
    ((0, 384), (384, 384), (768, 128)),
)


def md(a, n):
    return lax.rem(a, jnp.int32(n))


def dv(a, n):
    return lax.div(a, jnp.int32(n))


def dot(a, b, dims=((1,), (0,))):
    return lax.dot_general(a, b, (dims, ((), ())), preferred_element_type=F32)


def iota(shape, dim):
    return lax.broadcasted_iota(jnp.int32, shape, dim)


def window(start):
    block = dv(start, 128) - dv(start, 3000)
    return pl.multiple_of(block * 128, 128), start - block * 128


def kernel(
    patches_hbm,
    counts,
    owners,
    plan,
    gain,
    w1,
    bias1,
    w2t,
    bias2,
    scale2,
    out,
    patches,
    rows,
    own,
    stage,
    wall,
    normed,
    acc,
    loc_bias,
    hidden,
    part,
    pair,
    far,
    far_in,
    side,
    side_in,
    branch,
    encoded,
    going,
    coming,
    turned,
    l_sem,
    st_send,
    st_recv,
    y_send,
    y_recv,
    x_send,
    x_recv,
    c_send,
    c_recv,
    f_send,
    f_recv,
    s_send,
    s_recv,
    a_send,
    a_recv,
    b_send,
    b_recv,
):
    s = lax.axis_index("section")
    d = lax.axis_index("dp")
    q, c = dv(s, 2), md(s, 2)
    z, y, x = dv(d, 32), md(dv(d, 4), 8), md(d, 4)
    h = md(x + z, 2)
    e = md(x, 2)

    def dp_id(z_, y_, x_):
        return (s, z_ * 32 + y_ * 4 + x_)

    def peer(step):
        g = md(z * 4 + x + step, 8)
        return g, dv(g, 4), md(g, 4)

    def copy(src, dst, send, recv, device):
        return pltpu.make_async_remote_copy(
            src_ref=src,
            dst_ref=dst,
            send_sem=send,
            recv_sem=recv,
            device_id=device,
            device_id_type=MESH,
        )

    mate = (q * 2 + 1 - c, d)
    q_up = (md(q + 1, NQ) * 2 + c, d)
    q_dn = (md(q + NQ - 1, NQ) * 2 + c, d)

    load = pltpu.make_async_copy(patches_hbm, patches, l_sem)
    load.start()

    barrier = pltpu.get_barrier_semaphore()
    for step in range(1, 8):
        _, zp, xp = peer(step)
        for device in (dp_id(zp, y, xp), dp_id(z, md(y + step, 8), x)):
            pl.semaphore_signal(barrier, inc=1, device_id=device, device_id_type=MESH)
    for device in (mate, q_up, q_dn):
        pl.semaphore_signal(barrier, inc=1, device_id=device, device_id_type=MESH)

    own[...] = jnp.zeros_like(own)
    own[0, 0:SH, 0:FF] = w1[...]
    own[1, 0:SH, 0:FF] = w2t[...]

    pl.semaphore_wait(barrier, 17)

    def stage_copy(m, k, l):
        return copy(
            own.at[m],
            stage.at[m, x],
            st_send.at[m, 2 * k + l],
            st_recv.at[m, x],
            dp_id(md(z + l, 2), y, md(x + md(e + l, 2) + 2 * k, 4)),
        )

    def stage_start(m):
        for k in range(2):
            for l in range(2):
                if k or l:
                    stage_copy(m, k, l).start()
        pl.when(e == 1)(lambda: stage_copy(m, 0, 0).start())

        @pl.when(e == 0)
        def _():
            stage[m, x] = own[m]

    def stage_arrive(m, j):
        xs = md(x + j, 4)
        copy(own.at[m], stage.at[m, xs], st_send.at[m, 0], st_recv.at[m, xs], dp_id(z, y, x)).wait_recv()

    def stage_finish(m):
        pl.when(e == 1)(lambda: stage_arrive(m, 0))
        for j in range(1, 4):
            stage_arrive(m, j)
        row, col = iota((RUNP, 4 * SHP), 0), iota((RUNP, 4 * SHP), 1)
        pick = ((col == dv(row, SH) * SHP + md(row, SH)) & (row < RUN)).astype(BF16)
        wall[m, y, h] = dot(pick, stage[m].reshape(4 * SHP, FP)).astype(BF16)

    def y_copy(m, way, t, arriving=False):
        back = t + 1 if arriving else t
        b = md(y + 8 - back, 8) if way == 0 else md(y + back, 8)
        to = md(y + 1, 8) if way == 0 else md(y + 7, 8)
        start, size = (0, FP) if t < 3 else Y_CUTS[(way + m) % 2]
        ref = wall.at[m, b, h, :, pl.ds(start, size)]
        return copy(ref, ref, y_send.at[m, way, t], y_recv.at[m, way, t], dp_id(z, to, x))

    def x_copy(m, cut, b, arriving=False):
        to = dp_id(1 - z, y, x) if cut == 2 else dp_id(z, y, md(x + 1 + 2 * md(b + cut, 2), 4))
        half = 1 - h if arriving else h
        start, size = X_CUTS[m][cut]
        ref = wall.at[m, b, half, :, pl.ds(start, size)]
        return copy(ref, ref, x_send.at[m, cut, b], x_recv.at[m, cut, b], to)

    def block_at(way, t):
        return md(y + 8 - t, 8) if way == 0 else md(y + t, 8)

    def send_block(m, t):
        for way in range(2):
            if t > 0:
                y_copy(m, way, t - 1, True).wait_recv()
            if t < 4:
                y_copy(m, way, t).start()
            if t in (1, 2, 3):
                for cut in range(3):
                    x_copy(m, cut, block_at(way, t)).start()
        if t in (0, 4):
            for cut in range(3):
                x_copy(m, cut, block_at(0, t)).start()

    def each(t, use):
        def one(way, carry):
            use(md(y + way * t + (1 - way) * (8 - t), 8))
            return carry

        lax.fori_loop(0, 1 if t in (0, 4) else 2, one, 0)

    def x_arrive(m, b):
        for cut in range(3):
            x_copy(m, cut, b, True).wait_recv()

    def fc1(b):
        x_arrive(0, b)
        total = None
        for half in range(2):
            at, off = window(half * 1600 + b * RUN)
            row, col = iota((384, 2 * RUNP), 0), iota((384, 2 * RUNP), 1) - half * RUNP
            pick = ((row == col + off) & (col >= 0) & (col < RUN)).astype(BF16)
            term = dot(normed[:, pl.ds(at, 384)], pick)
            total = term if total is None else total + term
        acc[...] += dot(total.astype(BF16), wall[0, b].reshape(2 * RUNP, FP))

    def roles(b):
        rel = md(q + NQ - dv(b, 4), NQ)
        return c == md(dv(b, 2), 2), rel, dv(b, 4) * 2 + md(b, 2), md(b, 2)

    def pair_copy(b, slot):
        return copy(part.at[b], pair.at[slot], c_send.at[slot], c_recv.at[slot], mate)

    def far_copy(j, half):
        return copy(
            far.at[j, :, pl.ds(half * TOK, TOK)],
            far_in.at[j, half],
            f_send.at[j, half],
            f_recv.at[j, half],
            q_up if half else q_dn,
        )

    def side_copy(j, way):
        return copy(
            side.at[j, way], side_in.at[j, way], s_send.at[j, way], s_recv.at[j, way], q_up if way else q_dn
        )

    def fc2(b):
        x_arrive(1, b)
        term = dot(wall[1, b].reshape(2 * RUNP, FP), hidden[...], ((1,), (1,))).astype(BF16)
        part[b] = term.reshape(2, RUNP, ROWS)
        mine, _, slot, _ = roles(b)

        @pl.when(jnp.logical_not(mine))
        def _():
            pair_copy(b, slot).start()

    def both(b, slot, run):
        return part[b, run].astype(F32) + pair[slot, run].astype(F32)

    def sum_far(b):
        mine, rel, slot, j = roles(b)

        @pl.when(mine)
        def _():
            pair_copy(b, slot).wait_recv()

            @pl.when(md(rel, 2) == 0)
            def _():
                far[j] = both(b, slot, 1 - dv(rel, 2)).astype(BF16)
                for half in range(2):
                    far_copy(j, half).start()

    def sum_side(b):
        mine, rel, slot, j = roles(b)

        @pl.when(mine & (md(rel, 2) == 1))
        def _():
            for way in range(2):
                far_copy(j, way).wait_recv()
                run = dv(rel, 2) if way == 0 else 1 - dv(rel, 2)
                total = both(b, slot, run)
                lo, hi = total[:, 0:TOK], total[:, TOK:ROWS]
                if way == 0:
                    lo = lo + far_in[j, 0].astype(F32)
                else:
                    hi = hi + far_in[j, 1].astype(F32)
                side[j, way, :, 0:TOK] = lo.astype(BF16)
                side[j, way, :, TOK:ROWS] = hi.astype(BF16)
                side_copy(j, way).start()

    def sum_end(b):
        mine, rel, slot, j = roles(b)

        @pl.when(mine & (md(rel, 2) == 0))
        def _():
            for way in range(2):
                side_copy(j, way).wait_recv()
            total = both(b, slot, dv(rel, 2))
            branch[j] = total + side_in[j, 0].astype(F32) + side_in[j, 1].astype(F32)

    stage_start(0)
    stage_start(1)

    for i, ref in enumerate((gain, bias2, scale2)):
        rows[i : i + 1, :] = ref[...].reshape(1, D)

    stage_finish(0)
    send_block(0, 0)

    load.wait()

    def norm(i, carry):
        at = pl.ds(pl.multiple_of(i * 64, 64), 64)
        values = patches[at, :].astype(F32)
        scale = lax.rsqrt(jnp.mean(values * values, axis=1, keepdims=True) + 1e-06)
        normed[at, :] = (values * scale * rows[0:1, :]).astype(BF16)
        return carry

    lax.fori_loop(0, 8, norm, 0)
    acc[...] = jnp.zeros_like(acc)
    stage_finish(1)

    send_block(0, 1)
    each(0, fc1)
    send_block(0, 2)
    send_block(1, 0)
    each(1, fc1)

    loc_bias[...] = jnp.zeros_like(loc_bias)
    for k in range(4):
        held = jnp.zeros((1, SLOT), F32)
        for p in range(32):
            held = jnp.where(plan[k, s] == p, bias1[p * SLOT : (p + 1) * SLOT].reshape(1, SLOT), held)
        loc_bias[:, k * SLOT : (k + 1) * SLOT] = held

    send_block(0, 3)
    each(2, fc1)
    send_block(1, 1)
    send_block(0, 4)
    each(3, fc1)
    each(4, fc1)

    def gelu(i, carry):
        at = pl.ds(pl.multiple_of(i * 64, 64), 64)
        pre = acc[at, :] + loc_bias[...]
        hidden[at, :] = (0.5 * pre * (1.0 + lax.erf(pre * 0.7071067811865476))).astype(BF16)
        return carry

    lax.fori_loop(0, 8, gelu, 0)
    send_block(1, 2)
    each(0, fc2)
    each(1, fc2)
    each(0, sum_far)
    each(1, sum_far)

    owner_row = owners[...]
    eye = iota((TILES, TILES), 0) == iota((TILES, TILES), 1)
    owner = jnp.sum(jnp.where(eye, owner_row, 0).astype(F32), axis=1, keepdims=True).astype(jnp.int32)
    earlier = iota((TILES, TILES), 0) > iota((TILES, TILES), 1)
    rank = jnp.sum(((owner == owner_row) & earlier).astype(F32), axis=1, keepdims=True).astype(jnp.int32)
    tile = iota((TILES, 1), 0)
    count = jnp.zeros((TILES, 1), jnp.int32)
    for i in range(8):
        count = jnp.where(dv(tile, 8) == i, counts[i], count)
    place = md(dv(owner, 4), 8) * 128 + (dv(owner, 32) * 4 + md(owner, 4)) * 16 + rank * 8
    place = jnp.where(md(tile, 8) < count, place, -4096)
    token = iota((TILES, ROWS), 1)
    spread = jnp.where(iota((TILES, ROWS), 0) == dv(token, 8), place, 0).astype(F32)
    target = jnp.sum(spread, axis=0, keepdims=True).astype(jnp.int32) + md(iota((1, ROWS), 1), 8)

    send_block(1, 3)
    each(0, sum_side)
    each(2, fc2)
    each(2, sum_far)
    each(1, sum_side)
    send_block(1, 4)
    each(3, fc2)
    each(3, sum_far)
    each(0, sum_end)
    each(2, sum_side)
    each(4, fc2)
    each(4, sum_far)
    each(1, sum_end)
    each(3, sum_side)
    each(2, sum_end)
    each(4, sum_side)
    each(3, sum_end)
    each(4, sum_end)

    for j in range(2):
        at, off = window(s * FEAT + j * RUN)
        row, col = iota((RUNP, 384), 0), iota((RUNP, 384), 1)
        chosen = (col == row + off) & (row < RUN)
        values = dot(chosen.astype(BF16), patches[:, pl.ds(at, 384)], ((1,), (1,)))
        bias, scale = (
            jnp.sum(jnp.where(chosen, rows[i : i + 1, pl.ds(at, 384)], 0.0), axis=1, keepdims=True)
            for i in (1, 2)
        )
        encoded[j * RUNP : (j + 1) * RUNP] = (values + scale * (branch[j] + bias)).astype(BF16)

    def a_copy(step, arriving=False):
        to = md(y + step, 8)
        src = md(y + 8 - step, 8) if arriving else y
        return copy(going.at[to], coming.at[src], a_send.at[step], a_recv.at[step], dp_id(z, to, x))

    def put(step):
        to = md(y + step, 8)
        pick = (target == iota((128, ROWS), 0) + to * 128).astype(BF16)
        going[to] = dot(encoded[...], pick, ((1,), (1,))).astype(BF16)

    for step in (4, 3, 5, 2, 6, 1, 7):
        put(step)
        a_copy(step).start()
    put(0)

    row, col = iota((2 * RUNP, FEAT), 0), iota((2 * RUNP, FEAT), 1)
    keep = (row == col + jnp.where(col >= RUN, RUNP - RUN, 0)).astype(BF16)

    def b_copy(step, src, arriving=False):
        g, zp, xp = peer(8 - step) if arriving else peer(step)
        zo, xo = (zp, xp) if arriving else (z, x)
        return copy(
            turned.at[g, src], out.at[zo, src, xo], b_send.at[step, src], b_recv.at[step, src], dp_id(zp, y, xp)
        )

    def turn(src, block):
        turned[:, src] = dot(block, keep, ((0,), (0,))).astype(BF16).reshape(8, 16, FEAT)

        def send(step, carry):
            b_copy(step, src).start()
            return carry

        lax.fori_loop(1, 8, send, 0)

    turn(y, going[y])
    for step in (1, 7, 2, 6, 3, 5, 4):
        a_copy(step, True).wait_recv()
        src = md(y + 8 - step, 8)
        turn(src, coming[src])

    out[z, :, x] = turned[z * 4 + x]

    def finish(i, carry):
        step, src = dv(i, 8) + 1, md(i, 8)
        b_copy(step, src, True).wait_recv()
        b_copy(step, src).wait_send()
        return carry

    lax.fori_loop(0, 56, finish, 0)

    for m in range(2):
        for k in range(2):
            for l in range(2):
                if k or l:
                    stage_copy(m, k, l).wait_send()
        pl.when(e == 1)(lambda: stage_copy(m, 0, 0).wait_send())
        for way in range(2):
            for t in range(4):
                y_copy(m, way, t).wait_send()
        for cut in range(3):
            for b in range(8):
                x_copy(m, cut, b).wait_send()
    for slot in range(4):
        pair_copy(0, slot).wait_send()
    for j in range(2):
        for way in range(2):
            far_copy(j, way).wait_send()
            side_copy(j, way).wait_send()
    for step in range(1, 8):
        a_copy(step).wait_send()


def local(
    patches,
    tile_counts,
    owners,
    plan,
    norm_gain,
    fc1_weight,
    fc1_bias,
    fc2_weight,
    fc2_bias,
    layer_scale,
):
    width = patches.shape[2]
    vmem = pl.BlockSpec(memory_space=pltpu.VMEM)
    smem = pl.BlockSpec(memory_space=pltpu.SMEM)
    dma = pltpu.SemaphoreType.DMA
    received = pl.pallas_call(
        kernel,
        out_shape=jax.ShapeDtypeStruct((NZ, NY, NX, 16, FEAT), BF16),
        in_specs=[pl.BlockSpec(memory_space=pl.ANY), smem, vmem, smem] + [vmem] * 6,
        out_specs=vmem,
        scratch_shapes=[
            pltpu.VMEM((ROWS, D), BF16),
            pltpu.VMEM((8, D), F32),
            pltpu.VMEM((2, SHP, FP), BF16),
            pltpu.VMEM((2, 4, SHP, FP), BF16),
            pltpu.VMEM((2, 8, 2, RUNP, FP), BF16),
            pltpu.VMEM((ROWS, D), BF16),
            pltpu.VMEM((ROWS, FP), F32),
            pltpu.VMEM((1, FP), F32),
            pltpu.VMEM((ROWS, FP), BF16),
            pltpu.VMEM((8, 2, RUNP, ROWS), BF16),
            pltpu.VMEM((4, 2, RUNP, ROWS), BF16),
            pltpu.VMEM((2, RUNP, ROWS), BF16),
            pltpu.VMEM((2, 2, RUNP, TOK), BF16),
            pltpu.VMEM((2, 2, RUNP, ROWS), BF16),
            pltpu.VMEM((2, 2, RUNP, ROWS), BF16),
            pltpu.VMEM((2, RUNP, ROWS), F32),
            pltpu.VMEM((2 * RUNP, ROWS), BF16),
            pltpu.VMEM((8, 2 * RUNP, 128), BF16),
            pltpu.VMEM((8, 2 * RUNP, 128), BF16),
            pltpu.VMEM((8, 8, 16, FEAT), BF16),
            dma,
            dma((2, 4)),
            dma((2, 4)),
            dma((2, 2, 4)),
            dma((2, 2, 4)),
            dma((2, 3, 8)),
            dma((2, 3, 8)),
            dma((4,)),
            dma((4,)),
            dma((2, 2)),
            dma((2, 2)),
            dma((2, 2)),
            dma((2, 2)),
            dma((8,)),
            dma((8,)),
            dma((8, 8)),
            dma((8, 8)),
        ],
        compiler_params=pltpu.CompilerParams(
            collective_id=0, has_side_effects=True, vmem_limit_bytes=56 * 1024 * 1024
        ),
    )(
        patches.reshape(ROWS, width),
        tile_counts,
        owners.T,
        plan.T,
        norm_gain,
        fc1_weight,
        fc1_bias,
        fc2_weight.T,
        fc2_bias,
        layer_scale,
    )
    return received.reshape(NZ * NY * NX * 16, FEAT)


def solution(mesh):
    in_specs = (
        P("dp", None, None),
        P("dp"),
        P("dp", None),
        P(),
        P(),
        P("dp", "section"),
        P(),
        P("section", "dp"),
        P(),
        P(),
    )
    out_specs = P("dp", "section")
    return jax.shard_map(local, mesh=mesh, in_specs=in_specs, out_specs=out_specs, check_vma=False)
```

time: 197 us -> 159 us (0.81); the launches traced: 197 us -> 156 us
  Pallas kernels: 182 us -> 154 us
  local copies, waits for them, and re-layouts: 12.5 us -> 2.18 us
  other arithmetic: 2.49 us -> 0 us
    pallas_call x1, Pallas kernels: 182 us -> 154 us  [local(): pl.pallas_call(kernel, out_shape=jax.ShapeDtypeStruct((NZ, NY, NX, 16, FE...]
    reshape x4 -> x0, local copies, waits for them, and re-layouts: 2.58 us -> none  [the longest x1 1.32 us: local(): norm_gain.reshape(1, width)]
    unnamed x3 -> x0, local copies, waits for them, and re-layouts: 2.39 us -> none
    pad x3 -> x0, local copies, waits for them, and re-layouts: 2.02 us -> none  [the longest x2 1.42 us: mine(): return jnp.pad(held, ((0, 0), (0, RUNP - RUN), (0, 0)))]
where the time goes in v2:
time: 159 us; the launch traced here: 156 us
  Pallas kernels  154 us (97%)
  local copies, waits for them, and re-layouts  2.18 us (1%)
    pallas_call x1, Pallas kernels, local(): pl.pallas_call(kernel, out_shape=jax.ShapeDtypeStruct((NZ, NY, NX, 16, FE...  154 us

profile of v2, /device:TPU:6, one launch (start us, length us, event | category | flops | bytes accessed | tf_op | source)
XLA Modules:
  0.0 156.2 jit_solution(17307472807355707290)
XLA Ops:
  0.0 154.0 %shard_map.100 = bf16[2,8,4,16,400]{4,3,2,1,0:T(8,128)(2,1)} custom-call(bf16[512,3200]{1,0:T(8,128)(2,1)} %bitcast.6, s32[8]{0:T(128)} %counts.1, s32[1,64]{1,0:T(1,128)} %bitcast.9, s32[4,8]{1,0:T(4,128)} %bitcast.8, f32[3200]{0:T(1024)} %gain.1, bf16[50,800]{1,0:T(8,128)(2,1)} %w1.1, f32[6400]{0:T(1024)} %bias1.1, bf16[50,800]{1,0:T(8,128)(2,1)} %bitcast.7, ...), custom_call_target="tpu_custom_call" | custom-call | tf_op jit(solution)/shard_map/pallas_call | solution.py:496
  154.0 2.2 %copy.11 = bf16[1024,400]{0,1:T(8,128)(2,1)} copy(bf16[1024,400]{1,0:T(8,128)(2,1)} %bitcast.5) | data formatting | bytes 1638400 | tf_op jit(solution)/shard_map/reshape | solution.py:555

commit v3 on v2

v3 whole, which is shorter than its diff:
```python
import jax
import jax.numpy as jnp
from jax import lax
from jax.experimental import pallas as pl
from jax.experimental.pallas import tpu as pltpu
from jax.sharding import PartitionSpec as P

MESH = pl.DeviceIdType.MESH
F32 = jnp.float32
BF16 = jnp.bfloat16

NQ, NZ, NY, NX = 4, 2, 8, 4
D = 3200
FF = 800
FP = 896
SLOT = 200
SH = 50
SHP = 64
RUN = 200
RUNP = 208
FEAT = 400
ROWS = 512
TILES = 64
QUARTER = RUNP // 4
LAST = 6 * RUNP
PACKED = LAST + 64
HALF = PACKED // 2


def x_cuts(m, t):
    return ((0, 656), (656, 656)) if m == 1 and t > 1 else ((0, 432), (432, 432), (864, 448))


def md(a, n):
    return lax.rem(a, jnp.int32(n))


def dv(a, n):
    return lax.div(a, jnp.int32(n))


def dot(a, b, dims=((1,), (0,))):
    return lax.dot_general(a, b, (dims, ((), ())), preferred_element_type=F32)


def iota(shape, dim):
    return lax.broadcasted_iota(jnp.int32, shape, dim)


def window(start):
    block = dv(start, 128) - dv(start, 3000)
    return pl.multiple_of(block * 128, 128), start - block * 128


def kernel(
    patches_hbm,
    counts,
    owners,
    plan,
    gain,
    w1,
    bias1,
    w2t,
    bias2,
    scale2,
    out,
    patches,
    rows,
    own,
    stage,
    wall,
    flat,
    normed,
    acc,
    loc_bias,
    hidden,
    part,
    pair,
    far,
    side,
    sums_in,
    base,
    scales,
    picks,
    going,
    coming,
    turned,
    l_sem,
    st_send,
    st_recv,
    y_send,
    y_recv,
    x_send,
    x_recv,
    c_send,
    c_recv,
    s_send,
    s_recv,
    a_send,
    a_recv,
    b_send,
    b_recv,
):
    s = lax.axis_index("section")
    d = lax.axis_index("dp")
    q, c = dv(s, 2), md(s, 2)
    z, y, x = dv(d, 32), md(dv(d, 4), 8), md(d, 4)
    h = md(x + z, 2)
    e = md(x, 2)

    def dp_id(z_, y_, x_):
        return (s, z_ * 32 + y_ * 4 + x_)

    def peer(step):
        g = md(z * 4 + x + step, 8)
        return g, dv(g, 4), md(g, 4)

    def copy(src, dst, send, recv, device):
        return pltpu.make_async_remote_copy(
            src_ref=src,
            dst_ref=dst,
            send_sem=send,
            recv_sem=recv,
            device_id=device,
            device_id_type=MESH,
        )

    mate = (q * 2 + 1 - c, d)
    q_up = (md(q + 1, NQ) * 2 + c, d)
    q_dn = (md(q + NQ - 1, NQ) * 2 + c, d)
    q_far = (md(q + 2, NQ) * 2 + c, d)

    load = pltpu.make_async_copy(patches_hbm, patches, l_sem)
    load.start()

    barrier = pltpu.get_barrier_semaphore()
    for step in range(1, 8):
        _, zp, xp = peer(step)
        pl.semaphore_signal(barrier, inc=1, device_id=dp_id(zp, y, xp), device_id_type=MESH)
    for device in (dp_id(z, md(y + 1, 8), x), dp_id(z, md(y + 7, 8), x), mate, q_up, q_dn, q_far):
        pl.semaphore_signal(barrier, inc=1, device_id=device, device_id_type=MESH)

    own[...] = jnp.zeros_like(own)
    own[0, 0:SH, 0:FF] = w1[...]
    own[1, 0:SH, 0:FF] = w2t[...]

    pl.semaphore_wait(barrier, 13)

    quarters = dv(iota((RUNP, 128), 0), QUARTER) == dv(iota((RUNP, 128), 1), 32)

    def stage_copy(m, k, l):
        return copy(
            own.at[m],
            stage.at[m, x],
            st_send.at[m, 2 * k + l],
            st_recv.at[m, x],
            dp_id(md(z + l, 2), y, md(x + md(e + l, 2) + 2 * k, 4)),
        )

    def stage_start(m):
        for k in range(2):
            for l in range(2):
                if k or l:
                    stage_copy(m, k, l).start()
        pl.when(e == 1)(lambda: stage_copy(m, 0, 0).start())

        @pl.when(e == 0)
        def _():
            stage[m, x] = own[m]

    def stage_arrive(m, j):
        xs = md(x + j, 4)
        copy(own.at[m], stage.at[m, xs], st_send.at[m, 0], st_recv.at[m, xs], dp_id(z, y, x)).wait_recv()

    def stage_finish(m):
        pl.when(e == 1)(lambda: stage_arrive(m, 0))
        for j in range(1, 4):
            stage_arrive(m, j)
        row, col = iota((RUNP, 4 * SHP), 0), iota((RUNP, 4 * SHP), 1)
        pick = ((col == dv(row, SH) * SHP + md(row, SH)) & (row < RUN)).astype(BF16)
        whole = dot(pick, stage[m].reshape(4 * SHP, FP)).astype(BF16)
        for i in range(6):
            wall[m, y, h, i * RUNP : (i + 1) * RUNP, :] = whole[:, i * 128 : (i + 1) * 128]
        spread = (iota((128, 128), 0) == md(iota((128, 128), 1), 32)).astype(BF16)
        last = jnp.where(quarters, dot(whole[:, 768:FP], spread), 0.0).astype(BF16)
        fold = (iota((64, RUNP), 0) == md(iota((64, RUNP), 1), QUARTER)).astype(BF16)
        wall[m, y, h, LAST:PACKED, :] = dot(fold, last).astype(BF16)

    def unpack(m, b):
        for half in range(2):
            at = slice(half * RUNP, (half + 1) * RUNP)
            for i in range(6):
                flat[at, i * 128 : (i + 1) * 128] = wall[m, b, half, i * RUNP : (i + 1) * RUNP, :]
            unfold = (iota((RUNP, 64), 1) == md(iota((RUNP, 64), 0), QUARTER)).astype(BF16)
            last = jnp.where(quarters, dot(unfold, wall[m, b, half, LAST:PACKED, :]), 0.0).astype(BF16)
            gather = (md(iota((128, 128), 0), 32) == iota((128, 128), 1)).astype(BF16)
            flat[at, 768:FP] = dot(last, gather).astype(BF16)

    def y_copy(m, way, t, part, arriving=False):
        back = t + 1 if arriving else t
        b = md(y + 8 - back, 8) if way == 0 else md(y + back, 8)
        to = md(y + 1, 8) if way == 0 else md(y + 7, 8)
        ref = wall.at[m, b, h, pl.ds(part * HALF, HALF)]
        return copy(ref, ref, y_send.at[m, way, t, part], y_recv.at[m, way, t, part], dp_id(z, to, x))

    def x_copy(m, cut, b, t, arriving=False):
        to = (dp_id(z, y, md(x + 1, 4)), dp_id(z, y, md(x + 3, 4)), dp_id(1 - z, y, x))[cut]
        half = 1 - h if arriving else h
        start, size = x_cuts(m, t)[cut]
        ref = wall.at[m, b, half, pl.ds(start, size)]
        return copy(ref, ref, x_send.at[m, cut, b], x_recv.at[m, cut, b], to)

    def block_at(way, t):
        return md(y + 8 - t, 8) if way == 0 else md(y + t, 8)

    def y_parts(t):
        return [(way, part) for part in range(2) for way in range(2) if t < 3 or part == way]

    def send_y(m, t):
        if t == 0:
            for way, part in y_parts(0):
                y_copy(m, way, 0, part).start()
            return
        for way, part in y_parts(t - 1):
            y_copy(m, way, t - 1, part, True).wait_recv()
            if t < 4 and (way, part) in y_parts(t):
                y_copy(m, way, t, part).start()

    def send_x(m, t):
        for way in range(1 if t in (0, 4) else 2):
            for cut in range(len(x_cuts(m, t))):
                x_copy(m, cut, block_at(way, t), t).start()

    def send_block(m, t):
        send_y(m, t)
        send_x(m, t)

    def each(t, use):
        def one(way, carry):
            use(md(y + way * t + (1 - way) * (8 - t), 8), t)
            return carry

        lax.fori_loop(0, 1 if t in (0, 4) else 2, one, 0)

    def x_arrive(m, b, t):
        for cut in range(len(x_cuts(m, t))):
            x_copy(m, cut, b, t, True).wait_recv()

    def fc1(b, t):
        x_arrive(0, b, t)
        total = None
        for half in range(2):
            at, off = window(half * 1600 + b * RUN)
            row, col = iota((384, 2 * RUNP), 0), iota((384, 2 * RUNP), 1) - half * RUNP
            pick = ((row == col + off) & (col >= 0) & (col < RUN)).astype(BF16)
            term = dot(normed[:, pl.ds(at, 384)], pick)
            total = term if total is None else total + term
        unpack(0, b)
        acc[...] += dot(total.astype(BF16), flat[...])

    def roles(b):
        rel = md(q + NQ - dv(b, 4), NQ)
        return c == md(dv(b, 2), 2), rel, dv(b, 4) * 2 + md(b, 2), md(b, 2)

    def pair_copy(b, slot):
        return copy(part.at[b], pair.at[slot], c_send.at[slot], c_recv.at[slot], mate)

    def side_copy(j, way):
        to = q_up if way else q_dn
        return copy(side.at[j, way], sums_in.at[j, way], s_send.at[j, way], s_recv.at[j, way], to)

    def far_copy(j):
        return copy(far.at[j], sums_in.at[j, 2], s_send.at[j, 2], s_recv.at[j, 2], q_far)

    def fc2(b, t):
        x_arrive(1, b, t)
        unpack(1, b)
        term = dot(flat[...], hidden[...], ((1,), (1,))).astype(BF16)
        part[b] = term.reshape(2, RUNP, ROWS)
        mine, _, slot, _ = roles(b)

        @pl.when(jnp.logical_not(mine))
        def _():
            pair_copy(b, slot).start()

    def both(b, slot, run):
        return part[b, run].astype(F32) + pair[slot, run].astype(F32)

    def sum_send(b, t):
        mine, rel, slot, j = roles(b)

        @pl.when(mine)
        def _():
            pair_copy(b, slot).wait_recv()

            @pl.when(md(rel, 2) == 0)
            def _():
                far[j] = both(b, slot, 1 - dv(rel, 2)).astype(BF16)
                far_copy(j).start()

            @pl.when(md(rel, 2) == 1)
            def _():
                side[j, 0] = both(b, slot, dv(rel, 2)).astype(BF16)
                side_copy(j, 0).start()
                side[j, 1] = both(b, slot, 1 - dv(rel, 2)).astype(BF16)
                side_copy(j, 1).start()

    def sum_end(b, t):
        mine, rel, slot, j = roles(b)

        @pl.when(mine & (md(rel, 2) == 0))
        def _():
            total = both(b, slot, dv(rel, 2))
            for way in range(3):
                (far_copy(j) if way == 2 else side_copy(j, way)).wait_recv()
                total = total + sums_in[j, way].astype(F32)
            encoded = (base[j] + scales[j] * total).astype(BF16)
            for step in (4, 3, 5, 2, 6, 1, 7, 0):
                to = md(y + step, 8)
                going[j, to] = dot(encoded, picks[to], ((1,), (1,))).astype(BF16)
                if step:
                    a_copy(j, step).start()

    def a_copy(j, step, arriving=False):
        to = md(y + step, 8)
        src = md(y + 8 - step, 8) if arriving else y
        return copy(
            going.at[j, to], coming.at[j, src], a_send.at[j, step], a_recv.at[j, step], dp_id(z, to, x)
        )

    stage_start(0)

    for i, ref in enumerate((gain, bias2, scale2)):
        rows[i : i + 1, :] = ref[...].reshape(1, D)

    stage_finish(0)
    send_block(0, 0)
    stage_start(1)

    load.wait()

    def norm(i, carry):
        at = pl.ds(pl.multiple_of(i * 64, 64), 64)
        values = patches[at, :].astype(F32)
        scale = lax.rsqrt(jnp.mean(values * values, axis=1, keepdims=True) + 1e-06)
        normed[at, :] = (values * scale * rows[0:1, :]).astype(BF16)
        return carry

    lax.fori_loop(0, 8, norm, 0)
    acc[...] = jnp.zeros_like(acc)

    send_block(0, 1)
    each(0, fc1)
    stage_finish(1)

    loc_bias[...] = jnp.zeros_like(loc_bias)
    for k in range(4):
        held = jnp.zeros((1, SLOT), F32)
        for p in range(32):
            held = jnp.where(plan[k, s] == p, bias1[p * SLOT : (p + 1) * SLOT].reshape(1, SLOT), held)
        loc_bias[:, k * SLOT : (k + 1) * SLOT] = held

    send_block(0, 2)
    each(1, fc1)

    owner_row = owners[...]
    eye = iota((TILES, TILES), 0) == iota((TILES, TILES), 1)
    owner = jnp.sum(jnp.where(eye, owner_row, 0).astype(F32), axis=1, keepdims=True).astype(jnp.int32)
    earlier = iota((TILES, TILES), 0) > iota((TILES, TILES), 1)
    rank = jnp.sum(((owner == owner_row) & earlier).astype(F32), axis=1, keepdims=True).astype(jnp.int32)
    tile = iota((TILES, 1), 0)
    count = jnp.zeros((TILES, 1), jnp.int32)
    for i in range(8):
        count = jnp.where(dv(tile, 8) == i, counts[i], count)
    place = md(dv(owner, 4), 8) * 128 + (dv(owner, 32) * 4 + md(owner, 4)) * 16 + rank * 8
    place = jnp.where(md(tile, 8) < count, place, -4096)
    token = iota((TILES, ROWS), 1)
    spread = jnp.where(iota((TILES, ROWS), 0) == dv(token, 8), place, 0).astype(F32)
    target = jnp.sum(spread, axis=0, keepdims=True).astype(jnp.int32) + md(iota((1, ROWS), 1), 8)
    for to in range(8):
        picks[to] = (target == iota((128, ROWS), 0) + to * 128).astype(BF16)

    send_block(0, 3)
    send_y(1, 0)
    each(2, fc1)

    for j in range(2):
        at, off = window(s * FEAT + j * RUN)
        row, col = iota((RUNP, 384), 0), iota((RUNP, 384), 1)
        chosen = (col == row + off) & (row < RUN)
        values = dot(chosen.astype(BF16), patches[:, pl.ds(at, 384)], ((1,), (1,)))
        bias, scale = (
            jnp.sum(jnp.where(chosen, rows[i : i + 1, pl.ds(at, 384)], 0.0), axis=1, keepdims=True)
            for i in (1, 2)
        )
        base[j] = values + scale * bias
        scales[j] = scale

    send_block(0, 4)
    send_x(1, 0)
    each(3, fc1)
    each(4, fc1)
    send_block(1, 1)

    def gelu(i, carry):
        at = pl.ds(pl.multiple_of(i * 64, 64), 64)
        pre = acc[at, :] + loc_bias[...]
        hidden[at, :] = (0.5 * pre * (1.0 + lax.erf(pre * 0.7071067811865476))).astype(BF16)
        return carry

    lax.fori_loop(0, 8, gelu, 0)
    send_block(1, 2)
    each(0, fc2)
    each(1, fc2)
    each(0, sum_send)
    each(1, sum_send)
    send_block(1, 3)
    each(2, fc2)
    each(2, sum_send)
    send_block(1, 4)
    each(3, fc2)
    each(3, sum_send)
    each(4, fc2)
    each(4, sum_send)
    for t in range(5):
        each(t, sum_end)

    def b_copy(step, src, arriving=False):
        g, zp, xp = peer(8 - step) if arriving else peer(step)
        zo, xo = (zp, xp) if arriving else (z, x)
        return copy(
            turned.at[g, src], out.at[zo, src, xo], b_send.at[step, src], b_recv.at[step, src], dp_id(zp, y, xp)
        )

    def turn(src, held):
        block = None
        for j in range(2):
            keep = (iota((RUNP, FEAT), 1) == iota((RUNP, FEAT), 0) + j * RUN) & (iota((RUNP, FEAT), 0) < RUN)
            term = dot(held[j, src], keep.astype(BF16), ((0,), (0,)))
            block = term if block is None else block + term
        turned[:, src] = block.astype(BF16).reshape(8, 16, FEAT)

        def send(step, carry):
            b_copy(step, src).start()
            return carry

        lax.fori_loop(1, 8, send, 0)

    turn(y, going)
    for step in (1, 7, 2, 6, 3, 5, 4):
        for j in range(2):
            a_copy(j, step, True).wait_recv()
        turn(md(y + 8 - step, 8), coming)

    out[z, :, x] = turned[z * 4 + x]

    def finish(i, carry):
        step, src = dv(i, 8) + 1, md(i, 8)
        b_copy(step, src, True).wait_recv()
        b_copy(step, src).wait_send()
        return carry

    lax.fori_loop(0, 56, finish, 0)

    for m in range(2):
        for k in range(2):
            for l in range(2):
                if k or l:
                    stage_copy(m, k, l).wait_send()
        pl.when(e == 1)(lambda: stage_copy(m, 0, 0).wait_send())
        for t in range(4):
            for way, piece in y_parts(t):
                y_copy(m, way, t, piece).wait_send()
        for t in range(5):
            for way in range(1 if t in (0, 4) else 2):
                for cut in range(len(x_cuts(m, t))):
                    x_copy(m, cut, block_at(way, t), t).wait_send()
    for slot in range(4):
        pair_copy(0, slot).wait_send()
    for j in range(2):
        for way in range(2):
            side_copy(j, way).wait_send()
        far_copy(j).wait_send()
        for step in range(1, 8):
            a_copy(j, step).wait_send()


def local(
    patches,
    tile_counts,
    owners,
    plan,
    norm_gain,
    fc1_weight,
    fc1_bias,
    fc2_weight,
    fc2_bias,
    layer_scale,
):
    width = patches.shape[2]
    vmem = pl.BlockSpec(memory_space=pltpu.VMEM)
    smem = pl.BlockSpec(memory_space=pltpu.SMEM)
    dma = pltpu.SemaphoreType.DMA
    received = pl.pallas_call(
        kernel,
        out_shape=jax.ShapeDtypeStruct((NZ, NY, NX, 16, FEAT), BF16),
        in_specs=[pl.BlockSpec(memory_space=pl.ANY), smem, vmem, smem] + [vmem] * 6,
        out_specs=vmem,
        scratch_shapes=[
            pltpu.VMEM((ROWS, D), BF16),
            pltpu.VMEM((8, D), F32),
            pltpu.VMEM((2, SHP, FP), BF16),
            pltpu.VMEM((2, 4, SHP, FP), BF16),
            pltpu.VMEM((2, 8, 2, PACKED, 128), BF16),
            pltpu.VMEM((2 * RUNP, FP), BF16),
            pltpu.VMEM((ROWS, D), BF16),
            pltpu.VMEM((ROWS, FP), F32),
            pltpu.VMEM((1, FP), F32),
            pltpu.VMEM((ROWS, FP), BF16),
            pltpu.VMEM((8, 2, RUNP, ROWS), BF16),
            pltpu.VMEM((4, 2, RUNP, ROWS), BF16),
            pltpu.VMEM((2, RUNP, ROWS), BF16),
            pltpu.VMEM((2, 2, RUNP, ROWS), BF16),
            pltpu.VMEM((2, 3, RUNP, ROWS), BF16),
            pltpu.VMEM((2, RUNP, ROWS), F32),
            pltpu.VMEM((2, RUNP, 1), F32),
            pltpu.VMEM((8, 128, ROWS), BF16),
            pltpu.VMEM((2, 8, RUNP, 128), BF16),
            pltpu.VMEM((2, 8, RUNP, 128), BF16),
            pltpu.VMEM((8, 8, 16, FEAT), BF16),
            dma,
            dma((2, 4)),
            dma((2, 4)),
            dma((2, 2, 4, 2)),
            dma((2, 2, 4, 2)),
            dma((2, 3, 8)),
            dma((2, 3, 8)),
            dma((4,)),
            dma((4,)),
            dma((2, 3)),
            dma((2, 3)),
            dma((2, 8)),
            dma((2, 8)),
            dma((8, 8)),
            dma((8, 8)),
        ],
        compiler_params=pltpu.CompilerParams(
            collective_id=0, has_side_effects=True, vmem_limit_bytes=56 * 1024 * 1024
        ),
    )(
        patches.reshape(ROWS, width),
        tile_counts,
        owners.T,
        plan.T,
        norm_gain,
        fc1_weight,
        fc1_bias,
        fc2_weight.T,
        fc2_bias,
        layer_scale,
    )
    return received.reshape(NZ * NY * NX * 16, FEAT)


def solution(mesh):
    in_specs = (
        P("dp", None, None),
        P("dp"),
        P("dp", None),
        P(),
        P(),
        P("dp", "section"),
        P(),
        P("section", "dp"),
        P(),
        P(),
    )
    out_specs = P("dp", "section")
    return jax.shard_map(local, mesh=mesh, in_specs=in_specs, out_specs=out_specs, check_vma=False)
```

time: 159 us -> 145 us (0.912)
  the two profiles are of different devices: /device:TPU:6 before, /device:TPU:56 now
where the time goes in v3:
time: 145 us
  Pallas kernels  143 us (99%)
  local copies, waits for them, and re-layouts  2.18 us (2%)
    pallas_call x1, Pallas kernels, local(): pl.pallas_call(kernel, out_shape=jax.ShapeDtypeStruct((NZ, NY, NX, 16, FE...  143 us

profile of v3, /device:TPU:56, one launch (start us, length us, event | category | flops | bytes accessed | tf_op | source)
XLA Modules:
  0.0 144.9 jit_solution(9549760857580494476)
XLA Ops:
  0.0 142.7 %shard_map.100 = bf16[2,8,4,16,400]{4,3,2,1,0:T(8,128)(2,1)} custom-call(bf16[512,3200]{1,0:T(8,128)(2,1)} %bitcast.6, s32[8]{0:T(128)} %counts.1, s32[1,64]{1,0:T(1,128)} %bitcast.9, s32[4,8]{1,0:T(4,128)} %bitcast.8, f32[3200]{0:T(1024)} %gain.1, bf16[50,800]{1,0:T(8,128)(2,1)} %w1.1, f32[6400]{0:T(1024)} %bias1.1, bf16[50,800]{1,0:T(8,128)(2,1)} %bitcast.7, ...), custom_call_target="tpu_custom_call" | custom-call | tf_op jit(solution)/shard_map/pallas_call | solution.py:504
  142.7 2.2 %copy.11 = bf16[1024,400]{0,1:T(8,128)(2,1)} copy(bf16[1024,400]{1,0:T(8,128)(2,1)} %bitcast.5) | data formatting | bytes 1638400 | tf_op jit(solution)/shard_map/reshape | solution.py:562

commit v4 on v3

--- a/solution.py
+++ b/solution.py
@@ -27,8 +27,12 @@
 HALF = PACKED // 2
 
 
+def by_part(m, t):
+    return m == 1 and t > 1
+
+
 def x_cuts(m, t):
-    return ((0, 656), (656, 656)) if m == 1 and t > 1 else ((0, 432), (432, 432), (864, 448))
+    return ((0, HALF), (HALF, HALF)) if by_part(m, t) else ((0, 432), (432, 432), (864, 448))
 
 
 def md(a, n):
@@ -225,6 +229,8 @@
             y_copy(m, way, t - 1, part, True).wait_recv()
             if t < 4 and (way, part) in y_parts(t):
                 y_copy(m, way, t, part).start()
+            if by_part(m, t):
+                x_copy(m, part, block_at(way, t), t).start()
 
     def send_x(m, t):
         for way in range(1 if t in (0, 4) else 2):
@@ -233,7 +239,8 @@
 
     def send_block(m, t):
         send_y(m, t)
-        send_x(m, t)
+        if not by_part(m, t):
+            send_x(m, t)
 
     def each(t, use):
         def one(way, carry):
@@ -317,9 +324,12 @@
             encoded = (base[j] + scales[j] * total).astype(BF16)
             for step in (4, 3, 5, 2, 6, 1, 7, 0):
                 to = md(y + step, 8)
-                going[j, to] = dot(encoded, picks[to], ((1,), (1,))).astype(BF16)
+                placed = dot(encoded, picks[to], ((1,), (1,))).astype(BF16)
                 if step:
+                    going[j, to] = placed
                     a_copy(j, step).start()
+                else:
+                    coming[j, y] = placed
 
     def a_copy(j, step, arriving=False):
         to = md(y + step, 8)
@@ -418,12 +428,15 @@
     each(2, fc2)
     each(2, sum_send)
     send_block(1, 4)
+    each(0, sum_end)
+    each(1, sum_end)
     each(3, fc2)
     each(3, sum_send)
     each(4, fc2)
     each(4, sum_send)
-    for t in range(5):
-        each(t, sum_end)
+    each(2, sum_end)
+    each(3, sum_end)
+    each(4, sum_end)
 
     def b_copy(step, src, arriving=False):
         g, zp, xp = peer(8 - step) if arriving else peer(step)
@@ -432,11 +445,20 @@
             turned.at[g, src], out.at[zo, src, xo], b_send.at[step, src], b_recv.at[step, src], dp_id(zp, y, xp)
         )
 
-    def turn(src, held):
+    def turn(i, carry):
+        odd = md(i, 2)
+        src = md(2 * md(s, 4) + odd * dv(i + 1, 2) + (1 - odd) * (8 - dv(i, 2)), 8)
+        step = md(y + 8 - src, 8)
+
+        @pl.when(step > 0)
+        def _():
+            for j in range(2):
+                a_copy(j, step, True).wait_recv()
+
         block = None
         for j in range(2):
             keep = (iota((RUNP, FEAT), 1) == iota((RUNP, FEAT), 0) + j * RUN) & (iota((RUNP, FEAT), 0) < RUN)
-            term = dot(held[j, src], keep.astype(BF16), ((0,), (0,)))
+            term = dot(coming[j, src], keep.astype(BF16), ((0,), (0,)))
             block = term if block is None else block + term
         turned[:, src] = block.astype(BF16).reshape(8, 16, FEAT)
 
@@ -444,13 +466,9 @@
             b_copy(step, src).start()
             return carry
 
-        lax.fori_loop(1, 8, send, 0)
-
-    turn(y, going)
-    for step in (1, 7, 2, 6, 3, 5, 4):
-        for j in range(2):
-            a_copy(j, step, True).wait_recv()
-        turn(md(y + 8 - step, 8), coming)
+        return lax.fori_loop(1, 8, send, carry)
+
+    lax.fori_loop(0, 8, turn, 0)
 
     out[z, :, x] = turned[z * 4 + x]
 

time: 145 us -> 153 us (1.055)
  the two profiles are of different devices: /device:TPU:56 before, /device:TPU:6 now
where the time goes in v4:
time: 153 us; the launch traced here: 152 us
  Pallas kernels  150 us (98%)
  local copies, waits for them, and re-layouts  2.18 us (1%)
    pallas_call x1, Pallas kernels, local(): pl.pallas_call(kernel, out_shape=jax.ShapeDtypeStruct((NZ, NY, NX, 16, FE...  150 us

profile of v4, /device:TPU:6, one launch (start us, length us, event | category | flops | bytes accessed | tf_op | source)
XLA Modules:
  0.0 151.7 jit_solution(2054934140408710219)
XLA Ops:
  0.0 149.5 %shard_map.100 = bf16[2,8,4,16,400]{4,3,2,1,0:T(8,128)(2,1)} custom-call(bf16[512,3200]{1,0:T(8,128)(2,1)} %bitcast.6, s32[8]{0:T(128)} %counts.1, s32[1,64]{1,0:T(1,128)} %bitcast.9, s32[4,8]{1,0:T(4,128)} %bitcast.8, f32[3200]{0:T(1024)} %gain.1, bf16[50,800]{1,0:T(8,128)(2,1)} %w1.1, f32[6400]{0:T(1024)} %bias1.1, bf16[50,800]{1,0:T(8,128)(2,1)} %bitcast.7, ...), custom_call_target="tpu_custom_call" | custom-call | tf_op jit(solution)/shard_map/pallas_call | solution.py:522
  149.6 2.2 %copy.11 = bf16[1024,400]{0,1:T(8,128)(2,1)} copy(bf16[1024,400]{1,0:T(8,128)(2,1)} %bitcast.5) | data formatting | bytes 1638400 | tf_op jit(solution)/shard_map/reshape | solution.py:580

commit v5 on v4

--- a/solution.py
+++ b/solution.py
@@ -28,7 +28,7 @@
 
 
 def by_part(m, t):
-    return m == 1 and t > 1
+    return m == 1 and t > 2
 
 
 def x_cuts(m, t):
@@ -75,6 +75,7 @@
     wall,
     flat,
     normed,
+    acts,
     acc,
     loc_bias,
     hidden,
@@ -253,8 +254,7 @@
         for cut in range(len(x_cuts(m, t))):
             x_copy(m, cut, b, t, True).wait_recv()
 
-    def fc1(b, t):
-        x_arrive(0, b, t)
+    def act(b, t):
         total = None
         for half in range(2):
             at, off = window(half * 1600 + b * RUN)
@@ -262,8 +262,12 @@
             pick = ((row == col + off) & (col >= 0) & (col < RUN)).astype(BF16)
             term = dot(normed[:, pl.ds(at, 384)], pick)
             total = term if total is None else total + term
+        acts[b] = total.astype(BF16)
+
+    def fc1(b, t):
+        x_arrive(0, b, t)
         unpack(0, b)
-        acc[...] += dot(total.astype(BF16), flat[...])
+        acc[...] += dot(acts[b], flat[...])
 
     def roles(b):
         rel = md(q + NQ - dv(b, 4), NQ)
@@ -358,10 +362,12 @@
 
     lax.fori_loop(0, 8, norm, 0)
     acc[...] = jnp.zeros_like(acc)
+    each(0, act)
 
     send_block(0, 1)
     each(0, fc1)
     stage_finish(1)
+    each(1, act)
 
     loc_bias[...] = jnp.zeros_like(loc_bias)
     for k in range(4):
@@ -372,6 +378,9 @@
 
     send_block(0, 2)
     each(1, fc1)
+    each(2, act)
+    each(3, act)
+    each(4, act)
 
     owner_row = owners[...]
     eye = iota((TILES, TILES), 0) == iota((TILES, TILES), 1)
@@ -410,7 +419,6 @@
     send_x(1, 0)
     each(3, fc1)
     each(4, fc1)
-    send_block(1, 1)
 
     def gelu(i, carry):
         at = pl.ds(pl.multiple_of(i * 64, 64), 64)
@@ -418,67 +426,23 @@
         hidden[at, :] = (0.5 * pre * (1.0 + lax.erf(pre * 0.7071067811865476))).astype(BF16)
         return carry
 
-    lax.fori_loop(0, 8, gelu, 0)
+    lax.fori_loop(0, 4, gelu, 0)
+    send_block(1, 1)
+    lax.fori_loop(4, 8, gelu, 0)
+
+    each(0, fc2)
+    each(0, sum_send)
+    each(1, fc2)
     send_block(1, 2)
-    each(0, fc2)
-    each(1, fc2)
-    each(0, sum_send)
     each(1, sum_send)
     send_block(1, 3)
     each(2, fc2)
     each(2, sum_send)
     send_block(1, 4)
-    each(0, sum_end)
-    each(1, sum_end)
     each(3, fc2)
     each(3, sum_send)
     each(4, fc2)
     each(4, sum_send)
-    each(2, sum_end)
-    each(3, sum_end)
-    each(4, sum_end)
-
-    def b_copy(step, src, arriving=False):
-        g, zp, xp = peer(8 - step) if arriving else peer(step)
-        zo, xo = (zp, xp) if arriving else (z, x)
-        return copy(
-            turned.at[g, src], out.at[zo, src, xo], b_send.at[step, src], b_recv.at[step, src], dp_id(zp, y, xp)
-        )
-
-    def turn(i, carry):
-        odd = md(i, 2)
-        src = md(2 * md(s, 4) + odd * dv(i + 1, 2) + (1 - odd) * (8 - dv(i, 2)), 8)
-        step = md(y + 8 - src, 8)
-
-        @pl.when(step > 0)
-        def _():
-            for j in range(2):
-                a_copy(j, step, True).wait_recv()
-
-        block = None
-        for j in range(2):
-            keep = (iota((RUNP, FEAT), 1) == iota((RUNP, FEAT), 0) + j * RUN) & (iota((RUNP, FEAT), 0) < RUN)
-            term = dot(coming[j, src], keep.astype(BF16), ((0,), (0,)))
-            block = term if block is None else block + term
-        turned[:, src] = block.astype(BF16).reshape(8, 16, FEAT)
-
-        def send(step, carry):
-            b_copy(step, src).start()
-            return carry
-
-        return lax.fori_loop(1, 8, send, carry)
-
-    lax.fori_loop(0, 8, turn, 0)
-
-    out[z, :, x] = turned[z * 4 + x]
-
-    def finish(i, carry):
-        step, src = dv(i, 8) + 1, md(i, 8)
-        b_copy(step, src, True).wait_recv()
-        b_copy(step, src).wait_send()
-        return carry
-
-    lax.fori_loop(0, 56, finish, 0)
 
     for m in range(2):
         for k in range(2):
@@ -493,6 +457,49 @@
             for way in range(1 if t in (0, 4) else 2):
                 for cut in range(len(x_cuts(m, t))):
                     x_copy(m, cut, block_at(way, t), t).wait_send()
+
+    for t in range(5):
+        each(t, sum_end)
+
+    def b_copy(step, src):
+        g, zp, xp = peer(step)
+        return copy(turned.at[g, src], out.at[z, src, x], b_send.at[step], b_recv.at[step], dp_id(zp, y, xp))
+
+    def b_all(step):
+        g, zp, xp = peer(8 - step)
+        return copy(turned.at[g], out.at[zp, :, xp], b_send.at[step], b_recv.at[step], dp_id(zp, y, xp))
+
+    def turn(i, carry):
+        odd = md(i, 2)
+        src = md(2 * md(s, 4) + odd * dv(i + 1, 2) + (1 - odd) * (8 - dv(i, 2)), 8)
+        step = md(y + 8 - src, 8)
+
+        @pl.when(step > 0)
+        def _():
+            for j in range(2):
+                a_copy(j, step, True).wait_recv()
+
+        block = None
+        for j in range(2):
+            keep = (iota((RUNP, FEAT), 1) == iota((RUNP, FEAT), 0) + j * RUN) & (iota((RUNP, FEAT), 0) < RUN)
+            term = dot(coming[j, src], keep.astype(BF16), ((0,), (0,)))
+            block = term if block is None else block + term
+        turned[:, src] = block.astype(BF16).reshape(8, 16, FEAT)
+
+        def send(step, carry):
+            b_copy(step, src).start()
+            return carry
+
+        return lax.fori_loop(1, 8, send, carry)
+
+    lax.fori_loop(0, 8, turn, 0)
+
+    out[z, :, x] = turned[z * 4 + x]
+
+    for step in range(1, 8):
+        b_all(step).wait_recv()
+    for step in range(1, 8):
+        b_all(step).wait_send()
     for slot in range(4):
         pair_copy(0, slot).wait_send()
     for j in range(2):
@@ -532,6 +539,7 @@
             pltpu.VMEM((2, 8, 2, PACKED, 128), BF16),
             pltpu.VMEM((2 * RUNP, FP), BF16),
             pltpu.VMEM((ROWS, D), BF16),
+            pltpu.VMEM((8, ROWS, 2 * RUNP), BF16),
             pltpu.VMEM((ROWS, FP), F32),
             pltpu.VMEM((1, FP), F32),
             pltpu.VMEM((ROWS, FP), BF16),
@@ -559,8 +567,8 @@
             dma((2, 3)),
             dma((2, 8)),
             dma((2, 8)),
-            dma((8, 8)),
-            dma((8, 8)),
+            dma((8,)),
+            dma((8,)),
         ],
         compiler_params=pltpu.CompilerParams(
             collective_id=0, has_side_effects=True, vmem_limit_bytes=56 * 1024 * 1024

time: 153 us -> 138 us (0.902)
  Pallas kernels: 150 us -> 136 us
    pallas_call x1, Pallas kernels: 150 us -> 136 us  [local(): pl.pallas_call(kernel, out_shape=jax.ShapeDtypeStruct((NZ, NY, NX, 16, FE...]
where the time goes in v5:
time: 138 us
  Pallas kernels  136 us (99%)
  local copies, waits for them, and re-layouts  2.18 us (2%)
    pallas_call x1, Pallas kernels, local(): pl.pallas_call(kernel, out_shape=jax.ShapeDtypeStruct((NZ, NY, NX, 16, FE...  136 us

profile of v5, /device:TPU:6, one launch (start us, length us, event | category | flops | bytes accessed | tf_op | source)
XLA Modules:
  0.0 137.8 jit_solution(12740080169583395730)
XLA Ops:
  0.0 135.6 %shard_map.100 = bf16[2,8,4,16,400]{4,3,2,1,0:T(8,128)(2,1)} custom-call(bf16[512,3200]{1,0:T(8,128)(2,1)} %bitcast.6, s32[8]{0:T(128)} %counts.1, s32[1,64]{1,0:T(1,128)} %bitcast.9, s32[4,8]{1,0:T(4,128)} %bitcast.8, f32[3200]{0:T(1024)} %gain.1, bf16[50,800]{1,0:T(8,128)(2,1)} %w1.1, f32[6400]{0:T(1024)} %bias1.1, bf16[50,800]{1,0:T(8,128)(2,1)} %bitcast.7, ...), custom_call_target="tpu_custom_call" | custom-call | tf_op jit(solution)/shard_map/pallas_call | solution.py:529
  135.7 2.2 %copy.11 = bf16[1024,400]{0,1:T(8,128)(2,1)} copy(bf16[1024,400]{1,0:T(8,128)(2,1)} %bitcast.5) | data formatting | bytes 1638400 | tf_op jit(solution)/shard_map/reshape | solution.py:588

commit v6 on v5

--- a/solution.py
+++ b/solution.py
@@ -20,6 +20,8 @@
 RUNP = 208
 FEAT = 400
 ROWS = 512
+TOK = 256
+RELAYED = 1
 TILES = 64
 QUARTER = RUNP // 4
 LAST = 6 * RUNP
@@ -28,7 +30,7 @@
 
 
 def by_part(m, t):
-    return m == 1 and t > 2
+    return m == 1 and t > 1
 
 
 def x_cuts(m, t):
@@ -82,6 +84,7 @@
     part,
     pair,
     far,
+    far_in,
     side,
     sums_in,
     base,
@@ -90,6 +93,10 @@
     going,
     coming,
     turned,
+    quarters,
+    unfold,
+    gather,
+    keeps,
     l_sem,
     st_send,
     st_recv,
@@ -99,6 +106,8 @@
     x_recv,
     c_send,
     c_recv,
+    f_send,
+    f_recv,
     s_send,
     s_recv,
     a_send,
@@ -149,9 +158,15 @@
     own[0, 0:SH, 0:FF] = w1[...]
     own[1, 0:SH, 0:FF] = w2t[...]
 
+    quarters[...] = (dv(iota((RUNP, 128), 0), QUARTER) == dv(iota((RUNP, 128), 1), 32)).astype(F32)
+    unfold[...] = (iota((RUNP, 64), 1) == md(iota((RUNP, 64), 0), QUARTER)).astype(BF16)
+    gather[...] = (md(iota((128, 128), 0), 32) == iota((128, 128), 1)).astype(BF16)
+    for j in range(2):
+        row, col = iota((RUNP, FEAT), 0), iota((RUNP, FEAT), 1)
+        keeps[j] = ((col == row + j * RUN) & (row < RUN)).astype(BF16)
+
     pl.semaphore_wait(barrier, 13)
 
-    quarters = dv(iota((RUNP, 128), 0), QUARTER) == dv(iota((RUNP, 128), 1), 32)
 
     def stage_copy(m, k, l):
         return copy(
@@ -187,7 +202,7 @@
         for i in range(6):
             wall[m, y, h, i * RUNP : (i + 1) * RUNP, :] = whole[:, i * 128 : (i + 1) * 128]
         spread = (iota((128, 128), 0) == md(iota((128, 128), 1), 32)).astype(BF16)
-        last = jnp.where(quarters, dot(whole[:, 768:FP], spread), 0.0).astype(BF16)
+        last = (dot(whole[:, 768:FP], spread) * quarters[...]).astype(BF16)
         fold = (iota((64, RUNP), 0) == md(iota((64, RUNP), 1), QUARTER)).astype(BF16)
         wall[m, y, h, LAST:PACKED, :] = dot(fold, last).astype(BF16)
 
@@ -196,10 +211,8 @@
             at = slice(half * RUNP, (half + 1) * RUNP)
             for i in range(6):
                 flat[at, i * 128 : (i + 1) * 128] = wall[m, b, half, i * RUNP : (i + 1) * RUNP, :]
-            unfold = (iota((RUNP, 64), 1) == md(iota((RUNP, 64), 0), QUARTER)).astype(BF16)
-            last = jnp.where(quarters, dot(unfold, wall[m, b, half, LAST:PACKED, :]), 0.0).astype(BF16)
-            gather = (md(iota((128, 128), 0), 32) == iota((128, 128), 1)).astype(BF16)
-            flat[at, 768:FP] = dot(last, gather).astype(BF16)
+            last = (dot(unfold[...], wall[m, b, half, LAST:PACKED, :]) * quarters[...]).astype(BF16)
+            flat[at, 768:FP] = dot(last, gather[...]).astype(BF16)
 
     def y_copy(m, way, t, part, arriving=False):
         back = t + 1 if arriving else t
@@ -280,6 +293,15 @@
         to = q_up if way else q_dn
         return copy(side.at[j, way], sums_in.at[j, way], s_send.at[j, way], s_recv.at[j, way], to)
 
+    def near_copy(j, half):
+        return copy(
+            far.at[j, :, pl.ds(half * TOK, TOK)],
+            far_in.at[j, half],
+            f_send.at[j, half],
+            f_recv.at[j, half],
+            q_up if half else q_dn,
+        )
+
     def far_copy(j):
         return copy(far.at[j], sums_in.at[j, 2], s_send.at[j, 2], s_recv.at[j, 2], q_far)
 
@@ -307,14 +329,37 @@
             @pl.when(md(rel, 2) == 0)
             def _():
                 far[j] = both(b, slot, 1 - dv(rel, 2)).astype(BF16)
-                far_copy(j).start()
-
-            @pl.when(md(rel, 2) == 1)
-            def _():
-                side[j, 0] = both(b, slot, dv(rel, 2)).astype(BF16)
-                side_copy(j, 0).start()
-                side[j, 1] = both(b, slot, 1 - dv(rel, 2)).astype(BF16)
-                side_copy(j, 1).start()
+                if t > RELAYED:
+                    far_copy(j).start()
+                else:
+                    near_copy(j, 0).start()
+                    near_copy(j, 1).start()
+
+            if t > RELAYED:
+
+                @pl.when(md(rel, 2) == 1)
+                def _():
+                    side[j, 0] = both(b, slot, dv(rel, 2)).astype(BF16)
+                    side_copy(j, 0).start()
+                    side[j, 1] = both(b, slot, 1 - dv(rel, 2)).astype(BF16)
+                    side_copy(j, 1).start()
+
+    def sum_relay(b, t):
+        mine, rel, slot, j = roles(b)
+
+        @pl.when(mine & (md(rel, 2) == 1))
+        def _():
+            for way in range(2):
+                near_copy(j, way).wait_recv()
+                total = both(b, slot, dv(rel, 2) if way == 0 else 1 - dv(rel, 2))
+                lo, hi = total[:, 0:TOK], total[:, TOK:ROWS]
+                if way == 0:
+                    lo = lo + far_in[j, 0].astype(F32)
+                else:
+                    hi = hi + far_in[j, 1].astype(F32)
+                side[j, way, :, 0:TOK] = lo.astype(BF16)
+                side[j, way, :, TOK:ROWS] = hi.astype(BF16)
+                side_copy(j, way).start()
 
     def sum_end(b, t):
         mine, rel, slot, j = roles(b)
@@ -322,7 +367,7 @@
         @pl.when(mine & (md(rel, 2) == 0))
         def _():
             total = both(b, slot, dv(rel, 2))
-            for way in range(3):
+            for way in range(3 if t > RELAYED else 2):
                 (far_copy(j) if way == 2 else side_copy(j, way)).wait_recv()
                 total = total + sums_in[j, way].astype(F32)
             encoded = (base[j] + scales[j] * total).astype(BF16)
@@ -334,6 +379,11 @@
                     a_copy(j, step).start()
                 else:
                     coming[j, y] = placed
+            if t > RELAYED:
+                far_copy(j).wait_send()
+            else:
+                near_copy(j, 0).wait_send()
+                near_copy(j, 1).wait_send()
 
     def a_copy(j, step, arriving=False):
         to = md(y + step, 8)
@@ -431,17 +481,19 @@
     lax.fori_loop(4, 8, gelu, 0)
 
     each(0, fc2)
+    each(1, fc2)
     each(0, sum_send)
-    each(1, fc2)
     send_block(1, 2)
     each(1, sum_send)
+    each(0, sum_relay)
+    each(1, sum_relay)
     send_block(1, 3)
     each(2, fc2)
     each(2, sum_send)
     send_block(1, 4)
     each(3, fc2)
+    each(4, fc2)
     each(3, sum_send)
-    each(4, fc2)
     each(4, sum_send)
 
     for m in range(2):
@@ -481,8 +533,7 @@
 
         block = None
         for j in range(2):
-            keep = (iota((RUNP, FEAT), 1) == iota((RUNP, FEAT), 0) + j * RUN) & (iota((RUNP, FEAT), 0) < RUN)
-            term = dot(coming[j, src], keep.astype(BF16), ((0,), (0,)))
+            term = dot(coming[j, src], keeps[j], ((0,), (0,)))
             block = term if block is None else block + term
         turned[:, src] = block.astype(BF16).reshape(8, 16, FEAT)
 
@@ -505,7 +556,6 @@
     for j in range(2):
         for way in range(2):
             side_copy(j, way).wait_send()
-        far_copy(j).wait_send()
         for step in range(1, 8):
             a_copy(j, step).wait_send()
 
@@ -546,6 +596,7 @@
             pltpu.VMEM((8, 2, RUNP, ROWS), BF16),
             pltpu.VMEM((4, 2, RUNP, ROWS), BF16),
             pltpu.VMEM((2, RUNP, ROWS), BF16),
+            pltpu.VMEM((2, 2, RUNP, TOK), BF16),
             pltpu.VMEM((2, 2, RUNP, ROWS), BF16),
             pltpu.VMEM((2, 3, RUNP, ROWS), BF16),
             pltpu.VMEM((2, RUNP, ROWS), F32),
@@ -554,6 +605,10 @@
             pltpu.VMEM((2, 8, RUNP, 128), BF16),
             pltpu.VMEM((2, 8, RUNP, 128), BF16),
             pltpu.VMEM((8, 8, 16, FEAT), BF16),
+            pltpu.VMEM((RUNP, 128), F32),
+            pltpu.VMEM((RUNP, 64), BF16),
+            pltpu.VMEM((128, 128), BF16),
+            pltpu.VMEM((2, RUNP, FEAT), BF16),
             dma,
             dma((2, 4)),
             dma((2, 4)),
@@ -563,6 +618,8 @@
             dma((2, 3, 8)),
             dma((4,)),
             dma((4,)),
+            dma((2, 2)),
+            dma((2, 2)),
             dma((2, 3)),
             dma((2, 3)),
             dma((2, 8)),

time: 138 us -> 135 us (0.978); the launches traced: 138 us -> 133 us
  Pallas kernels: 136 us -> 131 us
    pallas_call x1, Pallas kernels: 136 us -> 131 us  [local(): pl.pallas_call(kernel, out_shape=jax.ShapeDtypeStruct((NZ, NY, NX, 16, FE...]
where the time goes in v6:
time: 135 us; the launch traced here: 133 us
  Pallas kernels  131 us (97%)
  local copies, waits for them, and re-layouts  2.18 us (2%)
    pallas_call x1, Pallas kernels, local(): pl.pallas_call(kernel, out_shape=jax.ShapeDtypeStruct((NZ, NY, NX, 16, FE...  131 us

profile of v6, /device:TPU:6, one launch (start us, length us, event | category | flops | bytes accessed | tf_op | source)
XLA Modules:
  0.0 133.2 jit_solution(2548484735900664876)
XLA Ops:
  0.0 131.0 %shard_map.100 = bf16[2,8,4,16,400]{4,3,2,1,0:T(8,128)(2,1)} custom-call(bf16[512,3200]{1,0:T(8,128)(2,1)} %bitcast.6, s32[8]{0:T(128)} %counts.1, s32[1,64]{1,0:T(1,128)} %bitcast.9, s32[4,8]{1,0:T(4,128)} %bitcast.8, f32[3200]{0:T(1024)} %gain.1, bf16[50,800]{1,0:T(8,128)(2,1)} %w1.1, f32[6400]{0:T(1024)} %bias1.1, bf16[50,800]{1,0:T(8,128)(2,1)} %bitcast.7, ...), custom_call_target="tpu_custom_call" | custom-call | tf_op jit(solution)/shard_map/pallas_call | solution.py:579
  131.0 2.2 %copy.11 = bf16[1024,400]{0,1:T(8,128)(2,1)} copy(bf16[1024,400]{1,0:T(8,128)(2,1)} %bitcast.5) | data formatting | bytes 1638400 | tf_op jit(solution)/shard_map/reshape | solution.py:645

commit v7 on v6

--- a/solution.py
+++ b/solution.py
@@ -21,7 +21,7 @@
 FEAT = 400
 ROWS = 512
 TOK = 256
-RELAYED = 1
+RELAYED = 2
 TILES = 64
 QUARTER = RUNP // 4
 LAST = 6 * RUNP
@@ -491,6 +491,7 @@
     each(2, fc2)
     each(2, sum_send)
     send_block(1, 4)
+    each(2, sum_relay)
     each(3, fc2)
     each(4, fc2)
     each(3, sum_send)

time: 135 us -> 142 us (1.052)
  Pallas kernels: 131 us -> 139 us
    pallas_call x1, Pallas kernels: 131 us -> 139 us  [local(): pl.pallas_call(kernel, out_shape=jax.ShapeDtypeStruct((NZ, NY, NX, 16, FE...]
where the time goes in v7:
time: 142 us; the launch traced here: 141 us
  Pallas kernels  139 us (98%)
  local copies, waits for them, and re-layouts  2.18 us (2%)
    pallas_call x1, Pallas kernels, local(): pl.pallas_call(kernel, out_shape=jax.ShapeDtypeStruct((NZ, NY, NX, 16, FE...  139 us

profile of v7, /device:TPU:6, one launch (start us, length us, event | category | flops | bytes accessed | tf_op | source)
XLA Modules:
  0.0 140.9 jit_solution(15842094100744465881)
XLA Ops:
  0.0 138.7 %shard_map.100 = bf16[2,8,4,16,400]{4,3,2,1,0:T(8,128)(2,1)} custom-call(bf16[512,3200]{1,0:T(8,128)(2,1)} %bitcast.6, s32[8]{0:T(128)} %counts.1, s32[1,64]{1,0:T(1,128)} %bitcast.9, s32[4,8]{1,0:T(4,128)} %bitcast.8, f32[3200]{0:T(1024)} %gain.1, bf16[50,800]{1,0:T(8,128)(2,1)} %w1.1, f32[6400]{0:T(1024)} %bias1.1, bf16[50,800]{1,0:T(8,128)(2,1)} %bitcast.7, ...), custom_call_target="tpu_custom_call" | custom-call | tf_op jit(solution)/shard_map/pallas_call | solution.py:580
  138.7 2.2 %copy.11 = bf16[1024,400]{0,1:T(8,128)(2,1)} copy(bf16[1024,400]{1,0:T(8,128)(2,1)} %bitcast.5) | data formatting | bytes 1638400 | tf_op jit(solution)/shard_map/reshape | solution.py:646
